TPU v7x, 32 devices: a whole 2x2x4 slice. The times are simulated.
32 devices in a mesh: req: 8 (over z, y), head: 4 (over x, core).
Axes of the slice: x: 2, y: 2, z: 4, core: 2. Of those that a mesh axis runs over, the one named last changes fastest.
Arguments:
- hidden_in: bfloat16 [128, 2048], P(None, 'req'), may hold values from -6 to 6
- lengths: int32 [128], P('req'), may hold values from 16 to 3072, as said below
- w_qkv: bfloat16 [3, 2048, 2048], P(None, 'req', 'head'), may hold values from -4 to 4, as said below
- qk_gain: float32 [2, 2048], P(None, 'head'), may hold values from 0.25 to 1.75
- cache_keys: bfloat16 [32768, 2048], P('req', 'head'), may hold values from -240 to 240
- cache_values: bfloat16 [32768, 2048], P('req', 'head'), may hold values from -6 to 6
- w_out: bfloat16 [2048, 2048], P('req', 'head'), may hold values from -3 to 3, as said below
- norm_gain: float32 [2, 2048], P(None, 'req'), may hold values from 0.25 to 1.75
- w_gate_up: bfloat16 [2, 2048, 8192], P(None, 'req', 'head'), may hold values from -0.125 to 0.125
- w_down: bfloat16 [2048, 8192], P('req', 'head'), may hold values from -3 to 3, as said below
Outputs:
- hidden_out: bfloat16 [128, 2048], P(None, 'req')
- new_keys: bfloat16 [128, 2048], P('req', 'head')
- new_values: bfloat16 [128, 2048], P('req', 'head')
Inputs may be any that keep to these rules, and one draw needn't show every extreme that they name: `lengths`: in each aligned group of requests 8 * 16 * k to 8 * 16 * k + 8 * 16 - 1 exactly one request, at a place drawn from the seed, has length 3072; every other length lies between 16 and 64. `w_qkv`: entries have magnitude at most 26 / sqrt(2048). `w_out`: entries have magnitude at most 23 / sqrt(2048). `w_down`: entries have magnitude at most 23 / sqrt(8192).
All inputs are finite; a program needn't handle non-finite values.
Results may differ from a plain program's by a relative error of at most 0.015.
Values may be sent and summed in bfloat16 or wider, within the bound.
A program may use at most 128 MiB of HBM per device.

v0:
```python
import jax
import jax.numpy as jnp
from jax import lax
from jax.sharding import PartitionSpec as P

HEAD_DIM = 128


EPS = 1e-06
THETA = 500000.0


def rotate(values, positions):
    half = values.shape[-1] // 2
    freqs = jnp.power(THETA, -(jnp.arange(half, dtype=jnp.float32) * 2.0 / values.shape[-1]))
    angles = positions.astype(jnp.float32)[:, None] * freqs[None, :]
    cosine = jnp.cos(angles)[:, None, :]
    sine = jnp.sin(angles)[:, None, :]
    first = values[..., :half]
    second = values[..., half:]
    return jnp.concatenate(
        [first * cosine - second * sine, second * cosine + first * sine], axis=-1
    )


def contract_last(left, right):
    return lax.dot_general(
        left, right, (((1,), (1,)), ((), ())), preferred_element_type=jnp.float32
    )


def body(
    hidden_in,
    lengths,
    w_qkv,
    qk_gain,
    cache_keys,
    cache_values,
    w_out,
    norm_gain,
    w_gate_up,
    w_down,
):
    rows_here = lengths.shape[0]
    width_here = w_qkv.shape[2]
    heads_here = width_here // HEAD_DIM
    units_here = w_gate_up.shape[2]
    full_width = width_here * lax.axis_size("head")
    model_width = hidden_in.shape[1] * lax.axis_size("req")
    selected = hidden_in
    product = jnp.einsum("bd,gdf->bgf", selected, w_qkv, preferred_element_type=jnp.float32)
    projected = lax.psum_scatter(
        product.reshape(rows_here * lax.axis_size("req"), 3 * width_here),
        "req",
        scatter_dimension=0,
        tiled=True,
    )
    query = projected[:, :width_here]
    key_new = projected[:, width_here : 2 * width_here]
    value_new = projected[:, 2 * width_here :].astype(jnp.bfloat16)
    query_squares, key_squares = lax.psum(
        (jnp.sum(query * query, axis=1), jnp.sum(key_new * key_new, axis=1)), "head"
    )
    query = query * lax.rsqrt(query_squares[:, None] / full_width + EPS) * qk_gain[0]
    key_new = key_new * lax.rsqrt(key_squares[:, None] / full_width + EPS) * qk_gain[1]
    query_rot = rotate(query.reshape(rows_here, heads_here, HEAD_DIM), lengths).astype(jnp.bfloat16)
    key_rot = rotate(key_new.reshape(rows_here, heads_here, HEAD_DIM), lengths).astype(jnp.bfloat16)
    value_heads = value_new.reshape(rows_here, heads_here, HEAD_DIM)
    scale = HEAD_DIM ** (-0.5)
    starts = jnp.cumsum(lengths) - lengths
    ends = starts + lengths
    own_score = jnp.sum(query_rot.astype(jnp.float32) * key_rot.astype(jnp.float32), axis=2) * scale
    pool_rows = cache_keys.shape[0]
    block = 512

    def attend_block(index, carry):
        running_max, running_total, running_sum = carry
        offset = index * block
        block_keys = lax.dynamic_slice_in_dim(cache_keys, offset, block, 0).reshape(
            block, heads_here, HEAD_DIM
        )
        block_values = lax.dynamic_slice_in_dim(cache_values, offset, block, 0).reshape(
            block, heads_here, HEAD_DIM
        )
        scores = (
            jnp.einsum("rhd,phd->rhp", query_rot, block_keys, preferred_element_type=jnp.float32)
            * scale
        )
        positions = offset + jnp.arange(block, dtype=jnp.int32)
        inside = (positions[None, :] >= starts[:, None]) & (positions[None, :] < ends[:, None])
        scores = jnp.where(inside[:, None, :], scores, -jnp.inf)
        new_max = jnp.maximum(running_max, jnp.max(scores, axis=2))
        weights = jnp.exp(scores - new_max[:, :, None]).astype(jnp.bfloat16)
        factor = jnp.exp(running_max - new_max)
        running_total = running_total * factor + jnp.sum(weights.astype(jnp.float32), axis=2)
        running_sum = running_sum * factor[:, :, None] + jnp.einsum(
            "rhp,phd->rhd", weights, block_values, preferred_element_type=jnp.float32
        )
        return (new_max, running_total, running_sum)

    steps_count = pool_rows // block
    initial = (own_score, jnp.ones_like(own_score), value_heads.astype(jnp.float32))
    final_max, final_total, final_sum = lax.fori_loop(0, steps_count, attend_block, initial)
    attended = (
        (final_sum / final_total[:, :, None]).astype(jnp.bfloat16).reshape(rows_here, width_here)
    )
    attn_part = contract_last(lax.all_gather(attended, "req", axis=0, tiled=True), w_out)
    attn_full = lax.psum(attn_part, "head")
    attn_power = lax.psum(jnp.sum(attn_full * attn_full, axis=1), "req")
    attn_normed = attn_full * lax.rsqrt(attn_power[:, None] / model_width + EPS) * norm_gain[0]
    hidden_mid = (hidden_in.astype(jnp.float32) + attn_normed).astype(jnp.bfloat16)
    selected = hidden_mid
    product = jnp.einsum("bd,gdf->bgf", selected, w_gate_up, preferred_element_type=jnp.float32)
    combined = lax.psum_scatter(
        product.reshape(rows_here * lax.axis_size("req"), 2 * units_here),
        "req",
        scatter_dimension=0,
        tiled=True,
    )
    gated = combined[:, :units_here]
    lifted = combined[:, units_here:]
    activated = (jax.nn.silu(gated) * lifted).astype(jnp.bfloat16)
    down_part = contract_last(lax.all_gather(activated, "req", axis=0, tiled=True), w_down)
    ffn_full = lax.psum(down_part, "head")
    ffn_power = lax.psum(jnp.sum(ffn_full * ffn_full, axis=1), "req")
    ffn_normed = ffn_full * lax.rsqrt(ffn_power[:, None] / model_width + EPS) * norm_gain[1]
    hidden_out = (hidden_mid.astype(jnp.float32) + ffn_normed).astype(jnp.bfloat16)
    return (hidden_out, key_rot.reshape(rows_here, width_here), value_new)


def solution(mesh):
    return jax.shard_map(
        body,
        mesh=mesh,
        in_specs=(
            P(None, "req"),
            P("req"),
            P(None, "req", "head"),
            P(None, "head"),
            P("req", "head"),
            P("req", "head"),
            P("req", "head"),
            P(None, "req"),
            P(None, "req", "head"),
            P("req", "head"),
        ),
        out_specs=(P(None, "req"), P("req", "head"), P("req", "head")),
        check_vma=False,
    )
```

profile of v0, /device:TPU:0, one launch (start us, length us, event | category | flops | bytes accessed | tf_op | source)
XLA Modules:
  0.0 376.7 jit_solution(7034813830735029840)
XLA Ops:
  7.2 1.7 fusion.7
  12.3 64.2 %reduce-scatter.7.cloned.1.call-done = f32[16,1536]{1,0:T(8,128)} async-done(((f32[128,1536]{1,0:T(8,128)}), f32[16,1536]{1,0:T(8,128)}) %reduce-scatter.7.cloned.1.call-update) | async-done | bytes 98320
  78.7 5.7 %all-reduce = (f32[16]{0:T(128)S(1)}, f32[16]{0:T(128)S(1)}) all-reduce(f32[16]{0:T(128)S(1)} %multiply_reduce_fusion, f32[16]{0:T(128)S(1)} %multiply_reduce_fusion.1), channel_id=1, replica_groups=mesh['req'=8,'head'=4] {'head'}, use_global_device_ids=true, to_apply=%region_4.0 | all-reduce | flops 32 | bytes 256 | tf_op jit(solution)/shard_map/psum | solution.py:61
  85.2 40.6 %while.18 = (s32[]{:T(128)}, f32[16,4]{0,1:T(4,128)S(1)}, f32[16,4]{0,1:T(4,128)S(1)}, f32[16,4,128]{2,0,1:T(8,128)S(1)}, s32[16]{0:T(128)}, /*index=5*/s32[16]{...) while((s32[]{:T(128)}, f32[16,4]{0,1:T(4,128)S(1)}, ...), condition=%wide.region_10.11_spmd.clone, body=%wide.region_7.10_spmd.clone.sunk | while | flops 17113800 | bytes 5742917 | solution.py:103
  88.3 1.3 fusion.39
  93.4 1.3 fusion.39
  96.2 1.3 constant_dynamic-slice_fusion.3
  98.5 1.3 fusion.39
  103.5 1.3 fusion.39
  108.6 1.3 fusion.39
  113.7 1.3 fusion.39
  118.8 1.3 fusion.39
  123.9 1.3 fusion.39
  126.0 30.5 %all_gather.6 = bf16[128,512]{1,0:T(8,128)(2,1)S(1)} all-gather(bf16[16,512]{1,0:T(8,128)(2,1)S(1)} %copy_bitcast_fusion.1), channel_id=1, replica_groups=mesh['req'=8,'head'=4] {'req'}, dimensions={0}, use_global_device_ids=true | all-gather | bytes 147456 | tf_op jit(solution)/shard_map/all_gather | solution.py:107
  156.5 1.8 fusion.17
  159.2 29.9 %all-reduce.4.cloned.1.call-done = f32[128,256]{1,0:T(8,128)} async-done(((f32[128,256]{1,0:T(8,128)}), f32[128,256]{1,0:T(8,128)}) %all-reduce.4.cloned.1.call-update) | async-done | bytes 131088 | tf_op jit(solution)/shard_map/psum | solution.py:108
  190.1 21.4 %psum.45 = f32[128]{0:T(128)S(1)} all-reduce(f32[128]{0:T(128)S(1)} %multiply_reduce_fusion.3), channel_id=1, replica_groups=mesh['req'=8,'head'=4] {'req'}, use_global_device_ids=true, to_apply=%region_13.14 | all-reduce | flops 128 | bytes 1024 | tf_op jit(solution)/shard_map/psum | solution.py:109
  212.5 2.3 fusion.5
  214.8 2.9 copy.74
  217.8 64.8 %reduce-scatter.9.cloned.1.call-done = f32[16,4096]{1,0:T(8,128)} async-done(((f32[128,4096]{1,0:T(8,128)}), f32[16,4096]{1,0:T(8,128)}) %reduce-scatter.9.cloned.1.call-update) | async-done | bytes 262160 | tf_op jit(solution)/shard_map/reduce_scatter | solution.py:114
  283.6 31.5 %all_gather.7 = bf16[128,2048]{1,0:T(8,128)(2,1)S(1)} all-gather(bf16[16,2048]{1,0:T(8,128)(2,1)S(1)} %fusion.4), channel_id=1, replica_groups=mesh['req'=8,'head'=4] {'req'}, dimensions={0}, use_global_device_ids=true | all-gather | bytes 589824 | tf_op jit(solution)/shard_map/all_gather | solution.py:123
  317.6 28.6 %all-reduce.6.cloned.1.call-done = f32[128,256]{1,0:T(8,128)} async-done(((f32[128,256]{1,0:T(8,128)}), f32[128,256]{1,0:T(8,128)}) %all-reduce.6.cloned.1.call-update) | async-done | bytes 131088 | tf_op jit(solution)/shard_map/psum | solution.py:124
  347.2 21.4 %psum.47 = f32[128]{0:T(128)S(1)} all-reduce(f32[128]{0:T(128)S(1)} %multiply_reduce_fusion.2), channel_id=1, replica_groups=mesh['req'=8,'head'=4] {'req'}, use_global_device_ids=true, to_apply=%region_17.18 | all-reduce | flops 128 | bytes 1024 | tf_op jit(solution)/shard_map/psum | solution.py:125
  368.6 1.6 add_convert_fusion
  (138 shorter events, 42.5 us)
Async XLA Ops:
  7.2 205.3 %copy-start = (bf16[2,256,2048]{2,1,0:T(8,128)(2,1)S(1)}, bf16[2,256,2048]{2,1,0:T(8,128)(2,1)}, u32[]{:S(2)}) copy-start(bf16[2,256,2048]{2,1,0:T(8,128)(2,1)} %param.20) | copy-start | bytes 6291460
  7.2 3.0 copy-start.4
  7.2 5.0 %copy-start.3 = (f32[2,512]{1,0:T(2,128)S(1)}, f32[2,512]{1,0:T(2,128)}, u32[]{:S(2)}) copy-start(f32[2,512]{1,0:T(2,128)} %param.15) | copy-start | bytes 12292
  7.2 69.3 %reduce-scatter.7.cloned.1.call-start = ((), (), s32[]{:S(2)}) async-start(), calls=%async_computation.4 | async-start | bytes 884736
  10.2 178.9 %all-reduce.4.cloned.1.call-start = ((), (), s32[]{:S(2)}) async-start(), calls=%async_computation.2 | async-start | bytes 262144 | tf_op jit(solution)/shard_map/psum | solution.py:108
  85.2 126.3 %copy-start.2 = (bf16[128,256]{1,0:T(8,128)(2,1)S(1)}, bf16[128,256]{1,0:T(8,128)(2,1)}, u32[]{:S(2)}) copy-start(bf16[128,256]{1,0:T(8,128)(2,1)} %param.12) | copy-start | bytes 196612
  158.4 124.2 %reduce-scatter.9.cloned.1.call-start = ((), (), s32[]{:S(2)}) async-start(), calls=%async_computation.5 | async-start | bytes 2359296 | tf_op jit(solution)/shard_map/reduce_scatter | solution.py:114
  217.7 97.4 %copy-start.1 = (bf16[256,2048]{1,0:T(8,128)(2,1)S(1)}, bf16[256,2048]{1,0:T(8,128)(2,1)}, u32[]{:S(2)}) copy-start(bf16[256,2048]{1,0:T(8,128)(2,1)} %param.21) | copy-start | bytes 3145732
  217.7 128.5 %all-reduce.6.cloned.1.call-start = ((), (), s32[]{:S(2)}) async-start(), calls=%async_computation.3 | async-start | bytes 262144 | tf_op jit(solution)/shard_map/psum | solution.py:124
Sparse Core Ops, SparseCore 0:
  11.3 65.0 reduce-scatter.6
  158.5 30.5 all-reduce.3
  217.8 64.6 reduce-scatter.8
  316.4 29.7 all-reduce.5
where the time goes:
time: 378 us; the launch traced here: 377 us
  waiting for transfers between devices  188 us (50%)
  blocking collectives  110 us (29%)
  local copies, waits for them, and re-layouts  28.6 us (8%)
  matrix products  19.6 us (5%)
  other arithmetic  16.1 us (4%)
  between operations  13.9 us (4%)
    reduce_scatter x1, waiting for transfers between devices, body(): lax.psum_scatter(product.reshape(rows_here * lax.axis_size('req'), 2 * un...  64.8 us
    unnamed x5, waiting for transfers between devices  64.2 us
    all_gather x1, blocking collectives, body(): lax.all_gather(activated, 'req', axis=0, tiled=True)  31.5 us
    all_gather x1, blocking collectives, body(): lax.all_gather(attended, 'req', axis=0, tiled=True)  30.5 us
    psum x1, waiting for transfers between devices, body(): attn_full = lax.psum(attn_part, 'head')  29.9 us
    psum x1, waiting for transfers between devices, body(): ffn_full = lax.psum(down_part, 'head')  28.6 us
    psum x1, blocking collectives, body(): attn_power = lax.psum(jnp.sum(attn_full * attn_full, axis=1), 'req')  21.4 us
    psum x1, blocking collectives, body(): ffn_power = lax.psum(jnp.sum(ffn_full * ffn_full, axis=1), 'req')  21.4 us
  transfers between devices with their start and end apart: 4, of which 4 were waited for; matrix products, arithmetic and copies ran while one was open for 1% of the time, Pallas kernels for 0%

commit v1 on v0

v1 whole, which is shorter than its diff:
```python
import functools

import jax
import jax.numpy as jnp
import numpy as np
from jax import lax
from jax.experimental import pallas as pl
from jax.experimental.pallas import tpu as pltpu
from jax.sharding import PartitionSpec as P

HEAD_DIM = 128
EPS = 1e-06
THETA = 500000.0
MESH = pl.DeviceIdType.MESH
F32 = jnp.float32
BF16 = jnp.bfloat16
CHUNKS = 4
KEY_BLOCK = 512


def dot(left, right):
    return lax.dot_general(left, right, (((1,), (0,)), ((), ())), preferred_element_type=F32)


def dot_last(left, right):
    return lax.dot_general(left, right, (((1,), (1,)), ((), ())), preferred_element_type=F32)


def kernel(
    n, heads_axis, model_width,
    lens, hid, qkg, ng, freq, wqkv_h, ck_h, cv_h, wout_h, wgu_h, wdn_h,
    out, nk, nv,
    wqkv, ck, cv, wout, wgu, wdn, load_sem,
    hp, pq, yq, sq, zq, pkv, ykv, skv, zkv, rs_send, rs_recv,
    sqs, sqr, sq_send, sq_recv,
    scores, att, att_send, att_recv,
    ar_src, ar_dst, ar_send, ar_recv,
    pw_src, pw_dst, pw_send, pw_recv,
    hm, gp, gy, gs, gz, gy_send, gy_recv, gz_send, gz_recv,
    act, az_send, az_recv, ay_send, ay_recv,
):
    me = lax.axis_index("req")
    hi = lax.axis_index("head")
    m = n // 2
    zi = lax.div(me, 2)
    yi = lax.rem(me, 2)
    rows = lens.shape[0]
    width = qkg.shape[1]
    heads = width // HEAD_DIM
    total_rows = n * rows
    slot = yi * m + zi
    ypart = zi * 2 + (1 - yi)

    def loader(index, src, dst):
        return pltpu.make_async_copy(src, dst, load_sem.at[index])

    loads = [
        loader(0, wqkv_h, wqkv), loader(1, ck_h, ck), loader(2, cv_h, cv),
        loader(3, wout_h, wout), loader(4, wgu_h, wgu), loader(5, wdn_h, wdn),
    ]
    for load in loads:
        load.start()

    barrier = pltpu.get_barrier_semaphore()
    for d in range(1, n):
        pl.semaphore_signal(barrier, inc=1, device_id=(lax.rem(me + d, n), hi), device_id_type=MESH)
    for d in range(1, heads_axis):
        pl.semaphore_signal(
            barrier, inc=1, device_id=(me, lax.rem(hi + d, heads_axis)), device_id_type=MESH
        )

    def send(src, dst, ssem, rsem, req, head):
        copy = pltpu.make_async_remote_copy(
            src_ref=src, dst_ref=dst, send_sem=ssem, recv_sem=rsem,
            device_id=(req, head), device_id_type=MESH,
        )
        copy.start()
        return copy

    pending = []

    for y in range(2):
        for z in range(m):
            hp[pl.ds((y * m + z) * rows, rows), :] = hid[pl.ds((z * 2 + y) * rows, rows), :]
    loads[0].wait()
    x = hp[...]
    pq[...] = dot(x, wqkv[0]).reshape(2, m, rows, width)
    pkv[:, :, :, :width] = dot(x, wqkv[1]).astype(BF16).reshape(2, m, rows, width)
    pkv[:, :, :, width:] = dot(x, wqkv[2]).astype(BF16).reshape(2, m, rows, width)
    pl.semaphore_wait(barrier, n - 1 + heads_axis - 1)
    yq_copy = send(pq.at[1 - yi], yq, rs_send.at[0, 0], rs_recv.at[0, 0], ypart, hi)
    ykv_copy = send(pkv.at[1 - yi], ykv, rs_send.at[1, 0], rs_recv.at[1, 0], ypart, hi)
    pending += [yq_copy, ykv_copy]

    row_id = lax.broadcasted_iota(jnp.int32, (rows, HEAD_DIM), 0)
    lane = lax.broadcasted_iota(jnp.int32, (rows, HEAD_DIM), 1)
    starts = jnp.zeros((rows, HEAD_DIM), jnp.int32)
    lengths = jnp.zeros((rows, HEAD_DIM), jnp.int32)
    at = jnp.int32(0)
    for r in range(rows):
        length = lens[r]
        starts = jnp.where(row_id == r, at, starts)
        lengths = jnp.where(row_id == r, length, lengths)
        at = at + length
    ends = starts + lengths
    angles = lengths.astype(F32) * freq[0:1, :]
    cosine = jnp.cos(angles)
    sine = jnp.sin(angles)
    sine = jnp.where(lane < HEAD_DIM // 2, -sine, sine)

    yq_copy.wait_recv()
    sq[...] = pq[yi] + yq[...]
    zq_copies = []
    for d in range(1, m):
        t = lax.rem(zi + d, m)
        zq_copies.append(
            send(sq.at[t], zq.at[d - 1], rs_send.at[0, d], rs_recv.at[0, d], t * 2 + yi, hi)
        )
    ykv_copy.wait_recv()
    skv[...] = (pkv[yi].astype(F32) + ykv[...].astype(F32)).astype(BF16)
    zkv_copies = []
    for d in range(1, m):
        t = lax.rem(zi + d, m)
        zkv_copies.append(
            send(skv.at[t], zkv.at[d - 1], rs_send.at[1, d], rs_recv.at[1, d], t * 2 + yi, hi)
        )
    pending += zq_copies + zkv_copies
    query = sq[zi]
    for d in range(1, m):
        zq_copies[d - 1].wait_recv()
        query = query + zq[d - 1]
    both = skv[zi].astype(F32)
    for d in range(1, m):
        zkv_copies[d - 1].wait_recv()
        both = both + zkv[d - 1].astype(F32)
    key_new = both[:, :width]
    value_new = both[:, width:].astype(BF16)
    nv[...] = value_new

    q_power = jnp.sum(query * query, axis=1, keepdims=True)
    k_power = jnp.sum(key_new * key_new, axis=1, keepdims=True)
    sqs[...] = jnp.where(lane < HEAD_DIM // 2, q_power, k_power)
    sq_copies = []
    for d in range(1, heads_axis):
        sq_copies.append(
            send(sqs, sqr.at[d - 1], sq_send.at[d - 1], sq_recv.at[d - 1],
                 me, lax.rem(hi + d, heads_axis))
        )
    pending += sq_copies
    powers = sqs[...]
    for d in range(1, heads_axis):
        sq_copies[d - 1].wait_recv()
        powers = powers + sqr[d - 1]
    full_width = width * heads_axis
    scales = lax.rsqrt(powers / full_width + EPS)
    query = query * scales[:, 0:1] * qkg[0:1, :]
    key_new = key_new * scales[:, HEAD_DIM - 1 : HEAD_DIM] * qkg[1:2, :]

    def rotate(values):
        parts = []
        for h in range(heads):
            part = values[:, h * HEAD_DIM : (h + 1) * HEAD_DIM]
            parts.append(part * cosine + pltpu.roll(part, HEAD_DIM // 2, 1) * sine)
        return jnp.concatenate(parts, axis=1)

    query_rot = rotate(query).astype(BF16).astype(F32)
    key_rot = rotate(key_new).astype(BF16)
    nk[...] = key_rot
    key_rot = key_rot.astype(F32)

    scale = HEAD_DIM ** (-0.5)
    wide_lane = lax.broadcasted_iota(jnp.int32, (rows, width), 1)
    q_rows = []
    own = []
    for h in range(heads):
        inside = (wide_lane >= h * HEAD_DIM) & (wide_lane < (h + 1) * HEAD_DIM)
        picked = jnp.where(inside, query_rot, 0.0)
        q_rows.append(picked)
        own.append(jnp.sum(picked * key_rot, axis=1, keepdims=True) * scale)
    q_rows = jnp.concatenate(q_rows, axis=0).astype(BF16)
    own = jnp.concatenate(own, axis=0)
    first = jnp.concatenate([starts[:, 0:1]] * heads, axis=0)
    last = jnp.concatenate([ends[:, 0:1]] * heads, axis=0)
    pool = ck.shape[0]
    loads[1].wait()
    highest = own
    for b in range(pool // KEY_BLOCK):
        span = pl.ds(b * KEY_BLOCK, KEY_BLOCK)
        s = dot_last(q_rows, ck[span, :]) * scale
        place = b * KEY_BLOCK + lax.broadcasted_iota(jnp.int32, s.shape, 1)
        s = jnp.where((place >= first) & (place < last), s, -1e30)
        scores[:, span] = s
        highest = jnp.maximum(highest, jnp.max(s, axis=1, keepdims=True))
    own_weight = jnp.exp(own - highest).astype(BF16).astype(F32)
    denominator = own_weight
    numerator = own_weight * jnp.concatenate([value_new.astype(F32)] * heads, axis=0)
    loads[2].wait()
    for b in range(pool // KEY_BLOCK):
        span = pl.ds(b * KEY_BLOCK, KEY_BLOCK)
        w = jnp.exp(scores[:, span] - highest).astype(BF16)
        denominator = denominator + jnp.sum(w.astype(F32), axis=1, keepdims=True)
        numerator = numerator + dot(w, cv[span, :])
    ratio = numerator / denominator
    attended = jnp.concatenate(
        [
            ratio[h * rows : (h + 1) * rows, h * HEAD_DIM : (h + 1) * HEAD_DIM]
            for h in range(heads)
        ],
        axis=1,
    ).astype(BF16)
    att[slot] = attended
    att_copies = []
    for d in range(1, n):
        t = lax.rem(me + d, n)
        att_copies.append(
            send(att.at[slot], att.at[slot], att_send.at[d - 1], att_recv.at[d - 1], t, hi)
        )
    pending += att_copies
    loads[3].wait()
    for d in range(1, n):
        s = lax.rem(me - d + n, n)
        there = att.at[lax.rem(s, 2) * m + lax.div(s, 2)]
        pltpu.make_async_remote_copy(
            src_ref=there, dst_ref=there, send_sem=att_send.at[d - 1],
            recv_sem=att_recv.at[d - 1], device_id=(s, hi), device_id_type=MESH,
        ).wait_recv()

    def sum_heads(part, which):
        bit = 1
        step = 0
        while bit < heads_axis:
            rounded = part.astype(BF16)
            ar_src[which, step] = rounded
            partner = hi + bit - 2 * bit * lax.rem(lax.div(hi, bit), 2)
            copy = send(ar_src.at[which, step], ar_dst.at[which, step],
                        ar_send.at[which, step], ar_recv.at[which, step], me, partner)
            pending.append(copy)
            copy.wait_recv()
            part = rounded.astype(F32) + ar_dst[which, step].astype(F32)
            bit *= 2
            step += 1
        return part

    eye = lax.broadcasted_iota(jnp.int32, (total_rows, total_rows), 0) == lax.broadcasted_iota(
        jnp.int32, (total_rows, total_rows), 1
    )

    def inverse_rms(part, which):
        power = jnp.sum(part * part, axis=1, keepdims=True)
        flat = jnp.sum(jnp.where(eye, power, 0.0), axis=0, keepdims=True)
        pw_src[which] = jnp.broadcast_to(flat, (8, total_rows))
        copies = []
        for d in range(1, n):
            copies.append(
                send(pw_src.at[which], pw_dst.at[which, d - 1], pw_send.at[which, d - 1],
                     pw_recv.at[which, d - 1], lax.rem(me + d, n), hi)
            )
        pending.extend(copies)
        for d in range(1, n):
            copies[d - 1].wait_recv()
            flat = flat + pw_dst[which, d - 1, 0:1, :]
        scaled = lax.rsqrt(flat / model_width + EPS)
        return jnp.sum(jnp.where(eye, scaled, 0.0), axis=1, keepdims=True)

    attn = sum_heads(dot_last(att[...].reshape(total_rows, width), wout[...]), 0)
    attn = attn * inverse_rms(attn, 0) * ng[0:1, :]
    hm[...] = (hp[...].astype(F32) + attn).astype(BF16)

    units = wgu.shape[2]
    cu = units // CHUNKS
    loads[4].wait()
    gy_copies = []
    for c in range(CHUNKS):
        cols = pl.ds(c * cu, cu)
        gp[c, :, :, :, :cu] = dot(hm[...], wgu[0, :, cols]).astype(BF16).reshape(2, m, rows, cu)
        gp[c, :, :, :, cu:] = dot(hm[...], wgu[1, :, cols]).astype(BF16).reshape(2, m, rows, cu)
        gy_copies.append(
            send(gp.at[c, 1 - yi], gy.at[c], gy_send.at[c], gy_recv.at[c], ypart, hi)
        )
    pending += gy_copies
    gz_copies = {}
    ay_copies = {}
    az_copies = {}
    state = {"down": None}

    def pair_sum(c):
        gy_copies[c].wait_recv()
        gs[c] = (gp[c, yi].astype(F32) + gy[c].astype(F32)).astype(BF16)
        for d in range(1, m):
            t = lax.rem(zi + d, m)
            gz_copies[c, d] = send(gs.at[c, t], gz.at[c, d - 1], gz_send.at[c, d - 1],
                                   gz_recv.at[c, d - 1], t * 2 + yi, hi)
            pending.append(gz_copies[c, d])

    def activate(c):
        full = gs[c, zi].astype(F32)
        for d in range(1, m):
            gz_copies[c, d].wait_recv()
            full = full + gz[c, d - 1].astype(F32)
        gate = full[:, :cu]
        act[c, slot] = (gate / (1.0 + jnp.exp(-gate)) * full[:, cu:]).astype(BF16)
        for d in range(1, m):
            t = lax.rem(zi + d, m)
            az_copies[c, d] = send(act.at[c, slot], act.at[c, slot], az_send.at[c, d - 1],
                                   az_recv.at[c, d - 1], t * 2 + yi, hi)
            pending.append(az_copies[c, d])

    def forward(c):
        for d in range(1, m):
            s = lax.rem(zi - d + m, m)
            there = act.at[c, yi * m + s]
            pltpu.make_async_remote_copy(
                src_ref=there, dst_ref=there, send_sem=az_send.at[c, d - 1],
                recv_sem=az_recv.at[c, d - 1], device_id=(s * 2 + yi, hi), device_id_type=MESH,
            ).wait_recv()
        mine = act.at[c, pl.ds(yi * m, m)]
        ay_copies[c] = send(mine, mine, ay_send.at[c], ay_recv.at[c], ypart, hi)
        pending.append(ay_copies[c])

    def project(c):
        other = act.at[c, pl.ds((1 - yi) * m, m)]
        pltpu.make_async_remote_copy(
            src_ref=other, dst_ref=other, send_sem=ay_send.at[c], recv_sem=ay_recv.at[c],
            device_id=(ypart, hi), device_id_type=MESH,
        ).wait_recv()
        if c == 0:
            loads[5].wait()
        part = dot_last(act[c].reshape(total_rows, cu), wdn[:, pl.ds(c * cu, cu)])
        state["down"] = part if state["down"] is None else state["down"] + part

    stages = (pair_sum, activate, forward, project)
    for step in range(CHUNKS + len(stages) - 1):
        for k, stage in enumerate(stages):
            if 0 <= step - k < CHUNKS:
                stage(step - k)
    ffn = sum_heads(state["down"], 1)
    ffn = ffn * inverse_rms(ffn, 1) * ng[1:2, :]
    result = (hm[...].astype(F32) + ffn).astype(BF16)
    for y in range(2):
        for z in range(m):
            p = (y * m + z) * rows
            out[pl.ds((z * 2 + y) * rows, rows), :] = result[p : p + rows]
    for copy in pending:
        copy.wait_send()


def body(
    n, heads_axis,
    hidden_in, lengths, w_qkv, qk_gain, cache_keys, cache_values,
    w_out, norm_gain, w_gate_up, w_down,
):
    rows = lengths.shape[0]
    total_rows, feat = hidden_in.shape
    width = w_qkv.shape[2]
    heads = width // HEAD_DIM
    units = w_gate_up.shape[2]
    m = n // 2
    cu = units // CHUNKS
    half = HEAD_DIM // 2
    steps = max(1, heads_axis.bit_length() - 1)
    freqs = np.power(THETA, -(np.arange(half, dtype=np.float64) * 2.0 / HEAD_DIM))
    freqs = np.broadcast_to(np.concatenate([freqs, freqs]), (8, HEAD_DIM)).astype(np.float32)
    dma = pltpu.SemaphoreType.DMA
    vmem = pltpu.VMEM
    scratch = [
        vmem(w_qkv.shape, BF16), vmem(cache_keys.shape, BF16), vmem(cache_values.shape, BF16),
        vmem(w_out.shape, BF16), vmem(w_gate_up.shape, BF16), vmem(w_down.shape, BF16), dma((6,)),
        vmem((total_rows, feat), BF16),
        vmem((2, m, rows, width), F32), vmem((m, rows, width), F32),
        vmem((m, rows, width), F32), vmem((m - 1, rows, width), F32),
        vmem((2, m, rows, 2 * width), BF16), vmem((m, rows, 2 * width), BF16),
        vmem((m, rows, 2 * width), BF16), vmem((m - 1, rows, 2 * width), BF16),
        dma((2, m)), dma((2, m)),
        vmem((rows, HEAD_DIM), F32), vmem((heads_axis - 1, rows, HEAD_DIM), F32),
        dma((heads_axis - 1,)), dma((heads_axis - 1,)),
        vmem((heads * rows, cache_keys.shape[0]), F32),
        vmem((n, rows, width), BF16), dma((n - 1,)), dma((n - 1,)),
        vmem((2, steps, total_rows, feat), BF16), vmem((2, steps, total_rows, feat), BF16),
        dma((2, steps)), dma((2, steps)),
        vmem((2, 8, total_rows), F32), vmem((2, n - 1, 8, total_rows), F32),
        dma((2, n - 1)), dma((2, n - 1)),
        vmem((total_rows, feat), BF16),
        vmem((CHUNKS, 2, m, rows, 2 * cu), BF16), vmem((CHUNKS, m, rows, 2 * cu), BF16),
        vmem((CHUNKS, m, rows, 2 * cu), BF16), vmem((CHUNKS, m - 1, rows, 2 * cu), BF16),
        dma((CHUNKS,)), dma((CHUNKS,)), dma((CHUNKS, m - 1)), dma((CHUNKS, m - 1)),
        vmem((CHUNKS, n, rows, cu), BF16),
        dma((CHUNKS, m - 1)), dma((CHUNKS, m - 1)), dma((CHUNKS,)), dma((CHUNKS,)),
    ]
    in_vmem = pl.BlockSpec(memory_space=pltpu.VMEM)
    anywhere = pl.BlockSpec(memory_space=pl.ANY)
    return pl.pallas_call(
        functools.partial(kernel, n, heads_axis, feat * n),
        out_shape=(
            jax.ShapeDtypeStruct((total_rows, feat), BF16),
            jax.ShapeDtypeStruct((rows, width), BF16),
            jax.ShapeDtypeStruct((rows, width), BF16),
        ),
        in_specs=[pl.BlockSpec(memory_space=pltpu.SMEM)] + [in_vmem] * 4 + [anywhere] * 6,
        out_specs=(in_vmem,) * 3,
        scratch_shapes=scratch,
        compiler_params=pltpu.CompilerParams(
            collective_id=0, has_side_effects=True, vmem_limit_bytes=56 * 1024 * 1024
        ),
    )(
        lengths, hidden_in, qk_gain, norm_gain, jnp.asarray(freqs),
        w_qkv, cache_keys, cache_values, w_out, w_gate_up, w_down,
    )


def solution(mesh):
    return jax.shard_map(
        functools.partial(body, mesh.shape["req"], mesh.shape["head"]),
        mesh=mesh,
        in_specs=(
            P(None, "req"),
            P("req"),
            P(None, "req", "head"),
            P(None, "head"),
            P("req", "head"),
            P("req", "head"),
            P("req", "head"),
            P(None, "req"),
            P(None, "req", "head"),
            P("req", "head"),
        ),
        out_specs=(P(None, "req"), P("req", "head"), P("req", "head")),
        check_vma=False,
    )
```

time: 378 us -> 81.4 us (0.22)
  waiting for transfers between devices: 188 us -> 0 us
  blocking collectives: 110 us -> 0 us
  Pallas kernels: 0 us -> 76.3 us
  local copies, waits for them, and re-layouts: 28.6 us -> 4.12 us
  matrix products: 19.6 us -> 0 us
  other arithmetic: 16.1 us -> 0 us
  between operations: 13.9 us -> 0.64 us
    pallas_call x0 -> x1, Pallas kernels: none -> 76.3 us  [body(): pl.pallas_call(functools.partial(kernel, n, heads_axis, feat * n), out_sh...]
    reduce_scatter x1 -> x0, waiting for transfers between devices: 64.8 us -> none  [body(): lax.psum_scatter(product.reshape(rows_here * lax.axis_size('req'), 2 * un...]
    unnamed x5 -> x0, waiting for transfers between devices: 64.2 us -> none
    all_gather x2 -> x0, blocking collectives: 62.1 us -> none  [the longest x1 31.5 us: body(): lax.all_gather(activated, 'req', axis=0, tiled=True)]
    psum x2 -> x0, waiting for transfers between devices: 58.5 us -> none  [the longest x1 29.9 us: body(): attn_full = lax.psum(attn_part, 'head')]
    psum x3 -> x0, blocking collectives: 48.4 us -> none  [the longest x1 21.4 us: body(): attn_power = lax.psum(jnp.sum(attn_full * attn_full, axis=1), 'req')]
    dynamic_slice x24 -> x0, local copies, waits for them, and re-layouts: 19.9 us -> none  [the longest x16 11.9 us: attend_block(): lax.dynamic_slice_in_dim(cache_values, offset, block, 0)]
    dot_general x20 -> x0, matrix products: 19.6 us -> none  [the longest x8 10.4 us: attend_block(): jnp.einsum('rhd,phd->rhp', query_rot, block_keys, preferred_element_type=...]
  transfers between devices with their start and end apart: 4 -> 0, of which waited for: 4 -> 0; matrix products, arithmetic and copies ran while one was open for 1% -> 0% of each run, Pallas kernels for 0% -> 0%
where the time goes in v1:
time: 81.4 us; the launch traced here: 81.1 us
  Pallas kernels  76.3 us (94%)
  local copies, waits for them, and re-layouts  4.12 us (5%)
    pallas_call x1, Pallas kernels, body(): pl.pallas_call(functools.partial(kernel, n, heads_axis, feat * n), out_sh...  76.3 us
    unnamed x3, local copies, waits for them, and re-layouts  4.12 us

profile of v1, /device:TPU:0, one launch (start us, length us, event | category | flops | bytes accessed | tf_op | source)
XLA Modules:
  0.0 81.1 jit_solution(12543458090251570104)
XLA Ops:
  0.6 76.3 %shard_map.130 = (bf16[128,256]{1,0:T(8,128)(2,1)}, bf16[16,512]{1,0:T(8,128)(2,1)}, bf16[16,512]{1,0:T(8,128)(2,1)}) custom-call(s32[16]{0:T(128)} %lens.1, bf16[128,256]{1,0:T(8,128)(2,1)} %hid.1, f32[2,512]{1,0:T(2,128)} %qkg.1, f32[2,256]{1,0:T(2,128)} %ng.1, f32[8,128]{1,0:T(8,128)} %constant.2.clone.freq, bf16[3,256,512]{2,1,0:T(8,128)(2,1)} %wqkv_h.1, ...), custom_call_target="tpu_custom_call" | custom-call | tf_op jit(solution)/shard_map/pallas_call | solution.py:391
  77.0 1.5 %copy.17 = bf16[128,256]{1,0:T(8,128)(2,1)} copy(bf16[128,256]{1,0:T(8,128)(2,1)} %get-tuple-element.6) | data formatting | bytes 131072
  78.4 1.3 %copy.18 = bf16[16,512]{1,0:T(8,128)(2,1)} copy(bf16[16,512]{1,0:T(8,128)(2,1)} %get-tuple-element.7) | data formatting | bytes 32768
  79.8 1.3 %copy.19 = bf16[16,512]{1,0:T(8,128)(2,1)} copy(bf16[16,512]{1,0:T(8,128)(2,1)} %get-tuple-element.8) | data formatting | bytes 32768

commit v2 on v1

--- a/solution.py
+++ b/solution.py
@@ -22,15 +22,20 @@
     return lax.dot_general(left, right, (((1,), (0,)), ((), ())), preferred_element_type=F32)
 
 
-def dot_last(left, right):
-    return lax.dot_general(left, right, (((1,), (1,)), ((), ())), preferred_element_type=F32)
+def place_outputs(a, b, c, out_a, out_b, out_c, sem):
+    pairs = ((a, out_a), (b, out_b), (c, out_c))
+    copies = [pltpu.make_async_copy(src, dst, sem.at[i]) for i, (src, dst) in enumerate(pairs)]
+    for copy in copies:
+        copy.start()
+    for copy in copies:
+        copy.wait()
 
 
 def kernel(
     n, heads_axis, model_width,
     lens, hid, qkg, ng, freq, wqkv_h, ck_h, cv_h, wout_h, wgu_h, wdn_h,
     out, nk, nv,
-    wqkv, ck, cv, wout, wgu, wdn, load_sem,
+    wqkv, ck, cv, wout, wgu, wdn, wout_t, wdn_t, load_sem,
     hp, pq, yq, sq, zq, pkv, ykv, skv, zkv, rs_send, rs_recv,
     sqs, sqr, sq_send, sq_recv,
     scores, att, att_send, att_recv,
@@ -58,8 +63,7 @@
         loader(0, wqkv_h, wqkv), loader(1, ck_h, ck), loader(2, cv_h, cv),
         loader(3, wout_h, wout), loader(4, wgu_h, wgu), loader(5, wdn_h, wdn),
     ]
-    for load in loads:
-        load.start()
+    loads[0].start()
 
     barrier = pltpu.get_barrier_semaphore()
     for d in range(1, n):
@@ -83,12 +87,14 @@
         for z in range(m):
             hp[pl.ds((y * m + z) * rows, rows), :] = hid[pl.ds((z * 2 + y) * rows, rows), :]
     loads[0].wait()
+    for load in loads[1:]:
+        load.start()
     x = hp[...]
     pq[...] = dot(x, wqkv[0]).reshape(2, m, rows, width)
+    pl.semaphore_wait(barrier, n - 1 + heads_axis - 1)
+    yq_copy = send(pq.at[1 - yi], yq, rs_send.at[0, 0], rs_recv.at[0, 0], ypart, hi)
     pkv[:, :, :, :width] = dot(x, wqkv[1]).astype(BF16).reshape(2, m, rows, width)
     pkv[:, :, :, width:] = dot(x, wqkv[2]).astype(BF16).reshape(2, m, rows, width)
-    pl.semaphore_wait(barrier, n - 1 + heads_axis - 1)
-    yq_copy = send(pq.at[1 - yi], yq, rs_send.at[0, 0], rs_recv.at[0, 0], ypart, hi)
     ykv_copy = send(pkv.at[1 - yi], ykv, rs_send.at[1, 0], rs_recv.at[1, 0], ypart, hi)
     pending += [yq_copy, ykv_copy]
 
@@ -125,10 +131,65 @@
             send(skv.at[t], zkv.at[d - 1], rs_send.at[1, d], rs_recv.at[1, d], t * 2 + yi, hi)
         )
     pending += zq_copies + zkv_copies
+    loads[3].wait()
+    wout_t[...] = wout[...].astype(F32).T.astype(BF16)
     query = sq[zi]
     for d in range(1, m):
         zq_copies[d - 1].wait_recv()
         query = query + zq[d - 1]
+
+    def share_power(values, which):
+        power = jnp.sum(values * values, axis=1, keepdims=True)
+        sqs[which] = jnp.broadcast_to(power, (rows, HEAD_DIM))
+        copies = []
+        for d in range(1, heads_axis):
+            copies.append(
+                send(sqs.at[which], sqr.at[which, d - 1], sq_send.at[which, d - 1],
+                     sq_recv.at[which, d - 1], me, lax.rem(hi + d, heads_axis))
+            )
+        pending.extend(copies)
+        return copies
+
+    def inverse_root(copies, which):
+        power = sqs[which]
+        for d in range(1, heads_axis):
+            copies[d - 1].wait_recv()
+            power = power + sqr[which, d - 1]
+        return lax.rsqrt(power[:, 0:1] / (width * heads_axis) + EPS)
+
+    def rotate(values):
+        parts = []
+        for h in range(heads):
+            part = values[:, h * HEAD_DIM : (h + 1) * HEAD_DIM]
+            parts.append(part * cosine + pltpu.roll(part, HEAD_DIM // 2, 1) * sine)
+        return jnp.concatenate(parts, axis=1)
+
+    q_copies = share_power(query, 0)
+    query = query * qkg[0:1, :]
+    query_rot = rotate(query * inverse_root(q_copies, 0)).astype(BF16).astype(F32)
+
+    scale = HEAD_DIM ** (-0.5)
+    wide_lane = lax.broadcasted_iota(jnp.int32, (rows, width), 1)
+    q_rows = []
+    for h in range(heads):
+        inside = (wide_lane >= h * HEAD_DIM) & (wide_lane < (h + 1) * HEAD_DIM)
+        q_rows.append(jnp.where(inside, query_rot, 0.0))
+    q_cols = jnp.concatenate(q_rows, axis=0).T.astype(BF16)
+    first = jnp.concatenate([starts[:, 0:1]] * heads, axis=0)
+    last = jnp.concatenate([ends[:, 0:1]] * heads, axis=0)
+    pool = ck.shape[0]
+    loads[1].wait()
+    highest = jnp.full((heads * rows, KEY_BLOCK), -1e30, F32)
+    column = lax.broadcasted_iota(jnp.int32, (heads * rows, KEY_BLOCK), 1)
+    for b in range(pool // KEY_BLOCK):
+        span = pl.ds(b * KEY_BLOCK, KEY_BLOCK)
+        s = dot(ck[span, :], q_cols).T * scale
+        place = b * KEY_BLOCK + column
+        s = jnp.where((place >= first) & (place < last), s, -1e30)
+        scores[:, span] = s
+        highest = jnp.maximum(highest, s)
+    highest = jnp.max(highest, axis=1, keepdims=True)
+
     both = skv[zi].astype(F32)
     for d in range(1, m):
         zkv_copies[d - 1].wait_recv()
@@ -136,70 +197,35 @@
     key_new = both[:, :width]
     value_new = both[:, width:].astype(BF16)
     nv[...] = value_new
-
-    q_power = jnp.sum(query * query, axis=1, keepdims=True)
-    k_power = jnp.sum(key_new * key_new, axis=1, keepdims=True)
-    sqs[...] = jnp.where(lane < HEAD_DIM // 2, q_power, k_power)
-    sq_copies = []
-    for d in range(1, heads_axis):
-        sq_copies.append(
-            send(sqs, sqr.at[d - 1], sq_send.at[d - 1], sq_recv.at[d - 1],
-                 me, lax.rem(hi + d, heads_axis))
-        )
-    pending += sq_copies
-    powers = sqs[...]
-    for d in range(1, heads_axis):
-        sq_copies[d - 1].wait_recv()
-        powers = powers + sqr[d - 1]
-    full_width = width * heads_axis
-    scales = lax.rsqrt(powers / full_width + EPS)
-    query = query * scales[:, 0:1] * qkg[0:1, :]
-    key_new = key_new * scales[:, HEAD_DIM - 1 : HEAD_DIM] * qkg[1:2, :]
-
-    def rotate(values):
-        parts = []
-        for h in range(heads):
-            part = values[:, h * HEAD_DIM : (h + 1) * HEAD_DIM]
-            parts.append(part * cosine + pltpu.roll(part, HEAD_DIM // 2, 1) * sine)
-        return jnp.concatenate(parts, axis=1)
-
-    query_rot = rotate(query).astype(BF16).astype(F32)
-    key_rot = rotate(key_new).astype(BF16)
-    nk[...] = key_rot
-    key_rot = key_rot.astype(F32)
-
-    scale = HEAD_DIM ** (-0.5)
-    wide_lane = lax.broadcasted_iota(jnp.int32, (rows, width), 1)
-    q_rows = []
-    own = []
-    for h in range(heads):
-        inside = (wide_lane >= h * HEAD_DIM) & (wide_lane < (h + 1) * HEAD_DIM)
-        picked = jnp.where(inside, query_rot, 0.0)
-        q_rows.append(picked)
-        own.append(jnp.sum(picked * key_rot, axis=1, keepdims=True) * scale)
-    q_rows = jnp.concatenate(q_rows, axis=0).astype(BF16)
-    own = jnp.concatenate(own, axis=0)
-    first = jnp.concatenate([starts[:, 0:1]] * heads, axis=0)
-    last = jnp.concatenate([ends[:, 0:1]] * heads, axis=0)
-    pool = ck.shape[0]
-    loads[1].wait()
-    highest = own
-    for b in range(pool // KEY_BLOCK):
-        span = pl.ds(b * KEY_BLOCK, KEY_BLOCK)
-        s = dot_last(q_rows, ck[span, :]) * scale
-        place = b * KEY_BLOCK + lax.broadcasted_iota(jnp.int32, s.shape, 1)
-        s = jnp.where((place >= first) & (place < last), s, -1e30)
-        scores[:, span] = s
-        highest = jnp.maximum(highest, jnp.max(s, axis=1, keepdims=True))
-    own_weight = jnp.exp(own - highest).astype(BF16).astype(F32)
-    denominator = own_weight
-    numerator = own_weight * jnp.concatenate([value_new.astype(F32)] * heads, axis=0)
+    k_copies = share_power(key_new, 1)
+
+    total = jnp.zeros((heads * rows, KEY_BLOCK), F32)
+    numerator = jnp.zeros((heads * rows, width), F32)
     loads[2].wait()
     for b in range(pool // KEY_BLOCK):
         span = pl.ds(b * KEY_BLOCK, KEY_BLOCK)
         w = jnp.exp(scores[:, span] - highest).astype(BF16)
-        denominator = denominator + jnp.sum(w.astype(F32), axis=1, keepdims=True)
+        total = total + w.astype(F32)
         numerator = numerator + dot(w, cv[span, :])
+    denominator = jnp.sum(total, axis=1, keepdims=True)
+
+    key_rot = rotate(key_new * inverse_root(k_copies, 1) * qkg[1:2, :]).astype(BF16)
+    nk[...] = key_rot
+    own = query_rot * key_rot.astype(F32)
+    own = jnp.concatenate(
+        [
+            jnp.sum(own[:, h * HEAD_DIM : (h + 1) * HEAD_DIM], axis=1, keepdims=True)
+            for h in range(heads)
+        ],
+        axis=0,
+    ) * scale
+    top = jnp.maximum(highest, own)
+    factor = jnp.exp(highest - top)
+    own_weight = jnp.exp(own - top).astype(BF16).astype(F32)
+    denominator = denominator * factor + own_weight
+    numerator = numerator * factor + own_weight * jnp.concatenate(
+        [value_new.astype(F32)] * heads, axis=0
+    )
     ratio = numerator / denominator
     attended = jnp.concatenate(
         [
@@ -216,7 +242,6 @@
             send(att.at[slot], att.at[slot], att_send.at[d - 1], att_recv.at[d - 1], t, hi)
         )
     pending += att_copies
-    loads[3].wait()
     for d in range(1, n):
         s = lax.rem(me - d + n, n)
         there = att.at[lax.rem(s, 2) * m + lax.div(s, 2)]
@@ -262,7 +287,7 @@
         scaled = lax.rsqrt(flat / model_width + EPS)
         return jnp.sum(jnp.where(eye, scaled, 0.0), axis=1, keepdims=True)
 
-    attn = sum_heads(dot_last(att[...].reshape(total_rows, width), wout[...]), 0)
+    attn = sum_heads(dot(att[...].reshape(total_rows, width), wout_t[...]), 0)
     attn = attn * inverse_rms(attn, 0) * ng[0:1, :]
     hm[...] = (hp[...].astype(F32) + attn).astype(BF16)
 
@@ -278,6 +303,8 @@
             send(gp.at[c, 1 - yi], gy.at[c], gy_send.at[c], gy_recv.at[c], ypart, hi)
         )
     pending += gy_copies
+    loads[5].wait()
+    wdn_t[...] = wdn[...].astype(F32).T.astype(BF16)
     gz_copies = {}
     ay_copies = {}
     az_copies = {}
@@ -323,9 +350,7 @@
             src_ref=other, dst_ref=other, send_sem=ay_send.at[c], recv_sem=ay_recv.at[c],
             device_id=(ypart, hi), device_id_type=MESH,
         ).wait_recv()
-        if c == 0:
-            loads[5].wait()
-        part = dot_last(act[c].reshape(total_rows, cu), wdn[:, pl.ds(c * cu, cu)])
+        part = dot(act[c].reshape(total_rows, cu), wdn_t[pl.ds(c * cu, cu), :])
         state["down"] = part if state["down"] is None else state["down"] + part
 
     stages = (pair_sum, activate, forward, project)
@@ -364,15 +389,16 @@
     vmem = pltpu.VMEM
     scratch = [
         vmem(w_qkv.shape, BF16), vmem(cache_keys.shape, BF16), vmem(cache_values.shape, BF16),
-        vmem(w_out.shape, BF16), vmem(w_gate_up.shape, BF16), vmem(w_down.shape, BF16), dma((6,)),
+        vmem(w_out.shape, BF16), vmem(w_gate_up.shape, BF16), vmem(w_down.shape, BF16),
+        vmem(w_out.shape[::-1], BF16), vmem(w_down.shape[::-1], BF16), dma((6,)),
         vmem((total_rows, feat), BF16),
         vmem((2, m, rows, width), F32), vmem((m, rows, width), F32),
         vmem((m, rows, width), F32), vmem((m - 1, rows, width), F32),
         vmem((2, m, rows, 2 * width), BF16), vmem((m, rows, 2 * width), BF16),
         vmem((m, rows, 2 * width), BF16), vmem((m - 1, rows, 2 * width), BF16),
         dma((2, m)), dma((2, m)),
-        vmem((rows, HEAD_DIM), F32), vmem((heads_axis - 1, rows, HEAD_DIM), F32),
-        dma((heads_axis - 1,)), dma((heads_axis - 1,)),
+        vmem((2, rows, HEAD_DIM), F32), vmem((2, heads_axis - 1, rows, HEAD_DIM), F32),
+        dma((2, heads_axis - 1)), dma((2, heads_axis - 1)),
         vmem((heads * rows, cache_keys.shape[0]), F32),
         vmem((n, rows, width), BF16), dma((n - 1,)), dma((n - 1,)),
         vmem((2, steps, total_rows, feat), BF16), vmem((2, steps, total_rows, feat), BF16),
@@ -388,7 +414,8 @@
     ]
     in_vmem = pl.BlockSpec(memory_space=pltpu.VMEM)
     anywhere = pl.BlockSpec(memory_space=pl.ANY)
-    return pl.pallas_call(
+    in_hbm = pl.BlockSpec(memory_space=pltpu.HBM)
+    outs = pl.pallas_call(
         functools.partial(kernel, n, heads_axis, feat * n),
         out_shape=(
             jax.ShapeDtypeStruct((total_rows, feat), BF16),
@@ -405,6 +432,13 @@
         lengths, hidden_in, qk_gain, norm_gain, jnp.asarray(freqs),
         w_qkv, cache_keys, cache_values, w_out, w_gate_up, w_down,
     )
+    return pl.pallas_call(
+        place_outputs,
+        out_shape=tuple(jax.ShapeDtypeStruct(a.shape, a.dtype) for a in outs),
+        in_specs=[in_hbm] * 3,
+        out_specs=(in_hbm,) * 3,
+        scratch_shapes=[dma((3,))],
+    )(*outs)
 
 
 def solution(mesh):

time: 81.4 us -> 82.1 us (level)
  Pallas kernels: 76.3 us -> 81.3 us
  local copies, waits for them, and re-layouts: 4.12 us -> 0 us
    unnamed x3 -> x0, local copies, waits for them, and re-layouts: 4.12 us -> none
    pallas_call x0 -> x1, Pallas kernels: none -> 4.11 us  [body(): pl.pallas_call(place_outputs, out_shape=tuple((jax.ShapeDtypeStruct(a.sha...]
    pallas_call x1, Pallas kernels: 76.3 us -> 77.2 us  [body(): pl.pallas_call(functools.partial(kernel, n, heads_axis, feat * n), out_sh...]
where the time goes in v2:
time: 82.1 us; the launch traced here: 81.9 us
  Pallas kernels  81.3 us (99%)
    pallas_call x1, Pallas kernels, body(): pl.pallas_call(functools.partial(kernel, n, heads_axis, feat * n), out_sh...  77.2 us
    pallas_call x1, Pallas kernels, body(): pl.pallas_call(place_outputs, out_shape=tuple((jax.ShapeDtypeStruct(a.sha...  4.11 us

profile of v2, /device:TPU:0, one launch (start us, length us, event | category | flops | bytes accessed | tf_op | source)
XLA Modules:
  0.0 81.9 jit_solution(1237135616109279170)
XLA Ops:
  0.6 77.2 %shard_map.130 = (bf16[128,256]{1,0:T(8,128)(2,1)}, bf16[16,512]{1,0:T(8,128)(2,1)}, bf16[16,512]{1,0:T(8,128)(2,1)}) custom-call(s32[16]{0:T(128)} %lens.1, bf16[128,256]{1,0:T(8,128)(2,1)} %hid.1, f32[2,512]{1,0:T(2,128)} %qkg.1, f32[2,256]{1,0:T(2,128)} %ng.1, f32[8,128]{1,0:T(8,128)} %constant.2.clone.freq, bf16[3,256,512]{2,1,0:T(8,128)(2,1)} %wqkv_h.1, ...), custom_call_target="tpu_custom_call" | custom-call | tf_op jit(solution)/shard_map/pallas_call | solution.py:418
  77.8 4.1 %shard_map.131 = (bf16[128,256]{1,0:T(8,128)(2,1)}, bf16[16,512]{1,0:T(8,128)(2,1)}, bf16[16,512]{1,0:T(8,128)(2,1)}) custom-call(bf16[128,256]{1,0:T(8,128)(2,1)} %get-tuple-element.6.a, bf16[16,512]{1,0:T(8,128)(2,1)} %get-tuple-element.7.b, bf16[16,512]{1,0:T(8,128)(2,1)} %get-tuple-element.8.c), custom_call_target="tpu_custom_call" | custom-call | tf_op jit(solution)/shard_map/pallas_call | solution.py:435

commit v3 on v2

--- a/solution.py
+++ b/solution.py
@@ -22,24 +22,22 @@
     return lax.dot_general(left, right, (((1,), (0,)), ((), ())), preferred_element_type=F32)
 
 
-def place_outputs(a, b, c, out_a, out_b, out_c, sem):
-    pairs = ((a, out_a), (b, out_b), (c, out_c))
-    copies = [pltpu.make_async_copy(src, dst, sem.at[i]) for i, (src, dst) in enumerate(pairs)]
-    for copy in copies:
-        copy.start()
-    for copy in copies:
-        copy.wait()
+def place_outputs(a, b, c, out_a, out_b, out_c):
+    out_a[...] = a[...]
+    out_b[...] = b[...]
+    out_c[...] = c[...]
 
 
 def kernel(
     n, heads_axis, model_width,
-    lens, hid, qkg, ng, freq, wqkv_h, ck_h, cv_h, wout_h, wgu_h, wdn_h,
+    lens, hid_h, qkg_h, ng_h, freq_h, wqkv_h, ck_h, cv_h, wout_h, wgu_h, wdn_h,
     out, nk, nv,
     wqkv, ck, cv, wout, wgu, wdn, wout_t, wdn_t, load_sem,
-    hp, pq, yq, sq, zq, pkv, ykv, skv, zkv, rs_send, rs_recv,
+    hid, qkg, ng, freq, small_sem,
+    hp, pq, zq, pkv, zkv, rs_send, rs_recv,
     sqs, sqr, sq_send, sq_recv,
     scores, att, att_send, att_recv,
-    ar_src, ar_dst, ar_send, ar_recv,
+    ar, ar_send, ar_recv,
     pw_src, pw_dst, pw_send, pw_recv,
     hm, gp, gy, gs, gz, gy_send, gy_recv, gz_send, gz_recv,
     act, az_send, az_recv, ay_send, ay_recv,
@@ -63,7 +61,14 @@
         loader(0, wqkv_h, wqkv), loader(1, ck_h, ck), loader(2, cv_h, cv),
         loader(3, wout_h, wout), loader(4, wgu_h, wgu), loader(5, wdn_h, wdn),
     ]
+    small_loads = [
+        pltpu.make_async_copy(src, dst, small_sem.at[i])
+        for i, (src, dst) in enumerate(((hid_h, hid), (qkg_h, qkg), (ng_h, ng), (freq_h, freq)))
+    ]
+    small_loads[0].start()
     loads[0].start()
+    for load in small_loads[1:]:
+        load.start()
 
     barrier = pltpu.get_barrier_semaphore()
     for d in range(1, n):
@@ -83,6 +88,7 @@
 
     pending = []
 
+    small_loads[0].wait()
     for y in range(2):
         for z in range(m):
             hp[pl.ds((y * m + z) * rows, rows), :] = hid[pl.ds((z * 2 + y) * rows, rows), :]
@@ -90,13 +96,32 @@
     for load in loads[1:]:
         load.start()
     x = hp[...]
-    pq[...] = dot(x, wqkv[0]).reshape(2, m, rows, width)
+    pq[...] = dot(x, wqkv[0]).astype(BF16).reshape(n, rows, width)
     pl.semaphore_wait(barrier, n - 1 + heads_axis - 1)
-    yq_copy = send(pq.at[1 - yi], yq, rs_send.at[0, 0], rs_recv.at[0, 0], ypart, hi)
-    pkv[:, :, :, :width] = dot(x, wqkv[1]).astype(BF16).reshape(2, m, rows, width)
-    pkv[:, :, :, width:] = dot(x, wqkv[2]).astype(BF16).reshape(2, m, rows, width)
-    ykv_copy = send(pkv.at[1 - yi], ykv, rs_send.at[1, 0], rs_recv.at[1, 0], ypart, hi)
-    pending += [yq_copy, ykv_copy]
+
+    def scatter(src, dst, which):
+        copies = []
+        for d in range(1, n):
+            t = lax.rem(me + d, n)
+            place = lax.rem(t, 2) * m + lax.div(t, 2)
+            copies.append(
+                send(src.at[place], dst.at[d - 1], rs_send.at[which, d - 1],
+                     rs_recv.at[which, d - 1], t, hi)
+            )
+        pending.extend(copies)
+        return copies
+
+    def gathered(src, dst, copies):
+        total = src[slot].astype(F32)
+        for d in range(1, n):
+            copies[d - 1].wait_recv()
+            total = total + dst[d - 1].astype(F32)
+        return total
+
+    zq_copies = scatter(pq, zq, 0)
+    pkv[:, :, :width] = dot(x, wqkv[1]).astype(BF16).reshape(n, rows, width)
+    pkv[:, :, width:] = dot(x, wqkv[2]).astype(BF16).reshape(n, rows, width)
+    zkv_copies = scatter(pkv, zkv, 1)
 
     row_id = lax.broadcasted_iota(jnp.int32, (rows, HEAD_DIM), 0)
     lane = lax.broadcasted_iota(jnp.int32, (rows, HEAD_DIM), 1)
@@ -109,34 +134,16 @@
         lengths = jnp.where(row_id == r, length, lengths)
         at = at + length
     ends = starts + lengths
+    small_loads[3].wait()
     angles = lengths.astype(F32) * freq[0:1, :]
     cosine = jnp.cos(angles)
     sine = jnp.sin(angles)
     sine = jnp.where(lane < HEAD_DIM // 2, -sine, sine)
 
-    yq_copy.wait_recv()
-    sq[...] = pq[yi] + yq[...]
-    zq_copies = []
-    for d in range(1, m):
-        t = lax.rem(zi + d, m)
-        zq_copies.append(
-            send(sq.at[t], zq.at[d - 1], rs_send.at[0, d], rs_recv.at[0, d], t * 2 + yi, hi)
-        )
-    ykv_copy.wait_recv()
-    skv[...] = (pkv[yi].astype(F32) + ykv[...].astype(F32)).astype(BF16)
-    zkv_copies = []
-    for d in range(1, m):
-        t = lax.rem(zi + d, m)
-        zkv_copies.append(
-            send(skv.at[t], zkv.at[d - 1], rs_send.at[1, d], rs_recv.at[1, d], t * 2 + yi, hi)
-        )
-    pending += zq_copies + zkv_copies
     loads[3].wait()
     wout_t[...] = wout[...].astype(F32).T.astype(BF16)
-    query = sq[zi]
-    for d in range(1, m):
-        zq_copies[d - 1].wait_recv()
-        query = query + zq[d - 1]
+    small_loads[1].wait()
+    query = gathered(pq, zq, zq_copies)
 
     def share_power(values, which):
         power = jnp.sum(values * values, axis=1, keepdims=True)
@@ -165,8 +172,7 @@
         return jnp.concatenate(parts, axis=1)
 
     q_copies = share_power(query, 0)
-    query = query * qkg[0:1, :]
-    query_rot = rotate(query * inverse_root(q_copies, 0)).astype(BF16).astype(F32)
+    query_rot = rotate(query * qkg[0:1, :]).astype(BF16).astype(F32)
 
     scale = HEAD_DIM ** (-0.5)
     wide_lane = lax.broadcasted_iota(jnp.int32, (rows, width), 1)
@@ -179,21 +185,19 @@
     last = jnp.concatenate([ends[:, 0:1]] * heads, axis=0)
     pool = ck.shape[0]
     loads[1].wait()
+    q_scale = jnp.concatenate([inverse_root(q_copies, 0) * scale] * heads, axis=0)
     highest = jnp.full((heads * rows, KEY_BLOCK), -1e30, F32)
     column = lax.broadcasted_iota(jnp.int32, (heads * rows, KEY_BLOCK), 1)
     for b in range(pool // KEY_BLOCK):
         span = pl.ds(b * KEY_BLOCK, KEY_BLOCK)
-        s = dot(ck[span, :], q_cols).T * scale
+        s = dot(ck[span, :], q_cols).T * q_scale
         place = b * KEY_BLOCK + column
         s = jnp.where((place >= first) & (place < last), s, -1e30)
         scores[:, span] = s
         highest = jnp.maximum(highest, s)
     highest = jnp.max(highest, axis=1, keepdims=True)
 
-    both = skv[zi].astype(F32)
-    for d in range(1, m):
-        zkv_copies[d - 1].wait_recv()
-        both = both + zkv[d - 1].astype(F32)
+    both = gathered(pkv, zkv, zkv_copies)
     key_new = both[:, :width]
     value_new = both[:, width:].astype(BF16)
     nv[...] = value_new
@@ -218,7 +222,7 @@
             for h in range(heads)
         ],
         axis=0,
-    ) * scale
+    ) * q_scale
     top = jnp.maximum(highest, own)
     factor = jnp.exp(highest - top)
     own_weight = jnp.exp(own - top).astype(BF16).astype(F32)
@@ -251,20 +255,26 @@
         ).wait_recv()
 
     def sum_heads(part, which):
-        bit = 1
-        step = 0
-        while bit < heads_axis:
-            rounded = part.astype(BF16)
-            ar_src[which, step] = rounded
-            partner = hi + bit - 2 * bit * lax.rem(lax.div(hi, bit), 2)
-            copy = send(ar_src.at[which, step], ar_dst.at[which, step],
-                        ar_send.at[which, step], ar_recv.at[which, step], me, partner)
-            pending.append(copy)
-            copy.wait_recv()
-            part = rounded.astype(F32) + ar_dst[which, step].astype(F32)
-            bit *= 2
-            step += 1
-        return part
+        held = ar.at[which]
+        held[hi] = part.astype(BF16)
+        copies = []
+        for d in range(1, heads_axis):
+            copies.append(
+                send(held.at[hi], held.at[hi], ar_send.at[which, d - 1],
+                     ar_recv.at[which, d - 1], me, lax.rem(hi + d, heads_axis))
+            )
+        pending.extend(copies)
+        for d in range(1, heads_axis):
+            there = held.at[lax.rem(hi - d + heads_axis, heads_axis)]
+            pltpu.make_async_remote_copy(
+                src_ref=there, dst_ref=there, send_sem=ar_send.at[which, d - 1],
+                recv_sem=ar_recv.at[which, d - 1],
+                device_id=(me, lax.rem(hi - d + heads_axis, heads_axis)), device_id_type=MESH,
+            ).wait_recv()
+        whole = held[0].astype(F32)
+        for h in range(1, heads_axis):
+            whole = whole + held[h].astype(F32)
+        return whole
 
     eye = lax.broadcasted_iota(jnp.int32, (total_rows, total_rows), 0) == lax.broadcasted_iota(
         jnp.int32, (total_rows, total_rows), 1
@@ -287,6 +297,7 @@
         scaled = lax.rsqrt(flat / model_width + EPS)
         return jnp.sum(jnp.where(eye, scaled, 0.0), axis=1, keepdims=True)
 
+    small_loads[2].wait()
     attn = sum_heads(dot(att[...].reshape(total_rows, width), wout_t[...]), 0)
     attn = attn * inverse_rms(attn, 0) * ng[0:1, :]
     hm[...] = (hp[...].astype(F32) + attn).astype(BF16)
@@ -382,7 +393,6 @@
     m = n // 2
     cu = units // CHUNKS
     half = HEAD_DIM // 2
-    steps = max(1, heads_axis.bit_length() - 1)
     freqs = np.power(THETA, -(np.arange(half, dtype=np.float64) * 2.0 / HEAD_DIM))
     freqs = np.broadcast_to(np.concatenate([freqs, freqs]), (8, HEAD_DIM)).astype(np.float32)
     dma = pltpu.SemaphoreType.DMA
@@ -391,18 +401,18 @@
         vmem(w_qkv.shape, BF16), vmem(cache_keys.shape, BF16), vmem(cache_values.shape, BF16),
         vmem(w_out.shape, BF16), vmem(w_gate_up.shape, BF16), vmem(w_down.shape, BF16),
         vmem(w_out.shape[::-1], BF16), vmem(w_down.shape[::-1], BF16), dma((6,)),
+        vmem(hidden_in.shape, BF16), vmem(qk_gain.shape, F32), vmem(norm_gain.shape, F32),
+        vmem((8, HEAD_DIM), F32), dma((4,)),
         vmem((total_rows, feat), BF16),
-        vmem((2, m, rows, width), F32), vmem((m, rows, width), F32),
-        vmem((m, rows, width), F32), vmem((m - 1, rows, width), F32),
-        vmem((2, m, rows, 2 * width), BF16), vmem((m, rows, 2 * width), BF16),
-        vmem((m, rows, 2 * width), BF16), vmem((m - 1, rows, 2 * width), BF16),
-        dma((2, m)), dma((2, m)),
+        vmem((n, rows, width), BF16), vmem((n - 1, rows, width), BF16),
+        vmem((n, rows, 2 * width), BF16), vmem((n - 1, rows, 2 * width), BF16),
+        dma((2, n - 1)), dma((2, n - 1)),
         vmem((2, rows, HEAD_DIM), F32), vmem((2, heads_axis - 1, rows, HEAD_DIM), F32),
         dma((2, heads_axis - 1)), dma((2, heads_axis - 1)),
         vmem((heads * rows, cache_keys.shape[0]), F32),
         vmem((n, rows, width), BF16), dma((n - 1,)), dma((n - 1,)),
-        vmem((2, steps, total_rows, feat), BF16), vmem((2, steps, total_rows, feat), BF16),
-        dma((2, steps)), dma((2, steps)),
+        vmem((2, heads_axis, total_rows, feat), BF16),
+        dma((2, heads_axis - 1)), dma((2, heads_axis - 1)),
         vmem((2, 8, total_rows), F32), vmem((2, n - 1, 8, total_rows), F32),
         dma((2, n - 1)), dma((2, n - 1)),
         vmem((total_rows, feat), BF16),
@@ -414,7 +424,6 @@
     ]
     in_vmem = pl.BlockSpec(memory_space=pltpu.VMEM)
     anywhere = pl.BlockSpec(memory_space=pl.ANY)
-    in_hbm = pl.BlockSpec(memory_space=pltpu.HBM)
     outs = pl.pallas_call(
         functools.partial(kernel, n, heads_axis, feat * n),
         out_shape=(
@@ -422,7 +431,7 @@
             jax.ShapeDtypeStruct((rows, width), BF16),
             jax.ShapeDtypeStruct((rows, width), BF16),
         ),
-        in_specs=[pl.BlockSpec(memory_space=pltpu.SMEM)] + [in_vmem] * 4 + [anywhere] * 6,
+        in_specs=[pl.BlockSpec(memory_space=pltpu.SMEM)] + [anywhere] * 10,
         out_specs=(in_vmem,) * 3,
         scratch_shapes=scratch,
         compiler_params=pltpu.CompilerParams(
@@ -435,9 +444,8 @@
     return pl.pallas_call(
         place_outputs,
         out_shape=tuple(jax.ShapeDtypeStruct(a.shape, a.dtype) for a in outs),
-        in_specs=[in_hbm] * 3,
-        out_specs=(in_hbm,) * 3,
-        scratch_shapes=[dma((3,))],
+        in_specs=[in_vmem] * 3,
+        out_specs=(in_vmem,) * 3,
     )(*outs)
 
 

time: 82.1 us -> 76.1 us (0.927)
  Pallas kernels: 81.3 us -> 75.2 us
    pallas_call x1, Pallas kernels: 77.2 us -> 73.7 us  [body(): pl.pallas_call(functools.partial(kernel, n, heads_axis, feat * n), out_sh...]
    pallas_call x1, Pallas kernels: 4.11 us -> 1.5 us  [body(): pl.pallas_call(place_outputs, out_shape=tuple((jax.ShapeDtypeStruct(a.sha...]
where the time goes in v3:
time: 76.1 us; the launch traced here: 75.9 us
  Pallas kernels  75.2 us (99%)
    pallas_call x1, Pallas kernels, body(): pl.pallas_call(functools.partial(kernel, n, heads_axis, feat * n), out_sh...  73.7 us

profile of v3, /device:TPU:0, one launch (start us, length us, event | category | flops | bytes accessed | tf_op | source)
XLA Modules:
  0.0 75.9 jit_solution(4118288087857443252)
XLA Ops:
  0.6 73.7 %shard_map.130 = (bf16[128,256]{1,0:T(8,128)(2,1)}, bf16[16,512]{1,0:T(8,128)(2,1)}, bf16[16,512]{1,0:T(8,128)(2,1)}) custom-call(s32[16]{0:T(128)} %lens.1, bf16[128,256]{1,0:T(8,128)(2,1)} %hid_h.1, f32[2,512]{1,0:T(2,128)} %qkg_h.1, f32[2,256]{1,0:T(2,128)} %ng_h.1, f32[8,128]{1,0:T(8,128)} %constant.2.clone.freq_h, bf16[3,256,512]{2,1,0:T(8,128)(2,1)} %wqkv_h.1, ...), custom_call_target="tpu_custom_call" | custom-call | tf_op jit(solution)/shard_map/pallas_call | solution.py:427
  74.4 1.5 %shard_map.131 = (bf16[128,256]{1,0:T(8,128)(2,1)}, bf16[16,512]{1,0:T(8,128)(2,1)}, bf16[16,512]{1,0:T(8,128)(2,1)}) custom-call(bf16[128,256]{1,0:T(8,128)(2,1)} %get-tuple-element.6.a, bf16[16,512]{1,0:T(8,128)(2,1)} %get-tuple-element.7.b, bf16[16,512]{1,0:T(8,128)(2,1)} %get-tuple-element.8.c), custom_call_target="tpu_custom_call" | custom-call | tf_op jit(solution)/shard_map/pallas_call | solution.py:444

commit v4 on v3

--- a/solution.py
+++ b/solution.py
@@ -14,7 +14,7 @@
 MESH = pl.DeviceIdType.MESH
 F32 = jnp.float32
 BF16 = jnp.bfloat16
-CHUNKS = 4
+CHUNKS = 8
 KEY_BLOCK = 512
 
 
@@ -34,7 +34,7 @@
     out, nk, nv,
     wqkv, ck, cv, wout, wgu, wdn, wout_t, wdn_t, load_sem,
     hid, qkg, ng, freq, small_sem,
-    hp, pq, zq, pkv, zkv, rs_send, rs_recv,
+    hp, pq, zq, pk, zk, pv, zv, rs_send, rs_recv,
     sqs, sqr, sq_send, sq_recv,
     scores, att, att_send, att_recv,
     ar, ar_send, ar_recv,
@@ -119,9 +119,10 @@
         return total
 
     zq_copies = scatter(pq, zq, 0)
-    pkv[:, :, :width] = dot(x, wqkv[1]).astype(BF16).reshape(n, rows, width)
-    pkv[:, :, width:] = dot(x, wqkv[2]).astype(BF16).reshape(n, rows, width)
-    zkv_copies = scatter(pkv, zkv, 1)
+    pk[...] = dot(x, wqkv[1]).astype(BF16).reshape(n, rows, width)
+    zk_copies = scatter(pk, zk, 1)
+    pv[...] = dot(x, wqkv[2]).astype(BF16).reshape(n, rows, width)
+    zv_copies = scatter(pv, zv, 2)
 
     row_id = lax.broadcasted_iota(jnp.int32, (rows, HEAD_DIM), 0)
     lane = lax.broadcasted_iota(jnp.int32, (rows, HEAD_DIM), 1)
@@ -197,10 +198,7 @@
         highest = jnp.maximum(highest, s)
     highest = jnp.max(highest, axis=1, keepdims=True)
 
-    both = gathered(pkv, zkv, zkv_copies)
-    key_new = both[:, :width]
-    value_new = both[:, width:].astype(BF16)
-    nv[...] = value_new
+    key_new = gathered(pk, zk, zk_copies)
     k_copies = share_power(key_new, 1)
 
     total = jnp.zeros((heads * rows, KEY_BLOCK), F32)
@@ -213,6 +211,8 @@
         numerator = numerator + dot(w, cv[span, :])
     denominator = jnp.sum(total, axis=1, keepdims=True)
 
+    value_new = gathered(pv, zv, zv_copies).astype(BF16)
+    nv[...] = value_new
     key_rot = rotate(key_new * inverse_root(k_copies, 1) * qkg[1:2, :]).astype(BF16)
     nk[...] = key_rot
     own = query_rot * key_rot.astype(F32)
@@ -246,6 +246,8 @@
             send(att.at[slot], att.at[slot], att_send.at[d - 1], att_recv.at[d - 1], t, hi)
         )
     pending += att_copies
+    loads[5].wait()
+    wdn_t[...] = wdn[...].astype(F32).T.astype(BF16)
     for d in range(1, n):
         s = lax.rem(me - d + n, n)
         there = att.at[lax.rem(s, 2) * m + lax.div(s, 2)]
@@ -314,8 +316,6 @@
             send(gp.at[c, 1 - yi], gy.at[c], gy_send.at[c], gy_recv.at[c], ypart, hi)
         )
     pending += gy_copies
-    loads[5].wait()
-    wdn_t[...] = wdn[...].astype(F32).T.astype(BF16)
     gz_copies = {}
     ay_copies = {}
     az_copies = {}
@@ -405,8 +405,9 @@
         vmem((8, HEAD_DIM), F32), dma((4,)),
         vmem((total_rows, feat), BF16),
         vmem((n, rows, width), BF16), vmem((n - 1, rows, width), BF16),
-        vmem((n, rows, 2 * width), BF16), vmem((n - 1, rows, 2 * width), BF16),
-        dma((2, n - 1)), dma((2, n - 1)),
+        vmem((n, rows, width), BF16), vmem((n - 1, rows, width), BF16),
+        vmem((n, rows, width), BF16), vmem((n - 1, rows, width), BF16),
+        dma((3, n - 1)), dma((3, n - 1)),
         vmem((2, rows, HEAD_DIM), F32), vmem((2, heads_axis - 1, rows, HEAD_DIM), F32),
         dma((2, heads_axis - 1)), dma((2, heads_axis - 1)),
         vmem((heads * rows, cache_keys.shape[0]), F32),

time: 76.1 us -> 80.4 us (1.057)
  Pallas kernels: 75.2 us -> 79.5 us
    pallas_call x1, Pallas kernels: 73.7 us -> 78 us  [body(): pl.pallas_call(functools.partial(kernel, n, heads_axis, feat * n), out_sh...]
where the time goes in v4:
time: 80.4 us; the launch traced here: 80.2 us
  Pallas kernels  79.5 us (99%)
    pallas_call x1, Pallas kernels, body(): pl.pallas_call(functools.partial(kernel, n, heads_axis, feat * n), out_sh...  78 us

profile of v4, /device:TPU:0, one launch (start us, length us, event | category | flops | bytes accessed | tf_op | source)
XLA Modules:
  0.0 80.2 jit_solution(4953505178012335515)
XLA Ops:
  0.6 78.0 %shard_map.130 = (bf16[128,256]{1,0:T(8,128)(2,1)}, bf16[16,512]{1,0:T(8,128)(2,1)}, bf16[16,512]{1,0:T(8,128)(2,1)}) custom-call(s32[16]{0:T(128)} %lens.1, bf16[128,256]{1,0:T(8,128)(2,1)} %hid_h.1, f32[2,512]{1,0:T(2,128)} %qkg_h.1, f32[2,256]{1,0:T(2,128)} %ng_h.1, f32[8,128]{1,0:T(8,128)} %constant.2.clone.freq_h, bf16[3,256,512]{2,1,0:T(8,128)(2,1)} %wqkv_h.1, ...), custom_call_target="tpu_custom_call" | custom-call | tf_op jit(solution)/shard_map/pallas_call | solution.py:428
  78.7 1.5 %shard_map.131 = (bf16[128,256]{1,0:T(8,128)(2,1)}, bf16[16,512]{1,0:T(8,128)(2,1)}, bf16[16,512]{1,0:T(8,128)(2,1)}) custom-call(bf16[128,256]{1,0:T(8,128)(2,1)} %get-tuple-element.6.a, bf16[16,512]{1,0:T(8,128)(2,1)} %get-tuple-element.7.b, bf16[16,512]{1,0:T(8,128)(2,1)} %get-tuple-element.8.c), custom_call_target="tpu_custom_call" | custom-call | tf_op jit(solution)/shard_map/pallas_call | solution.py:445

commit v5 on v3

--- a/solution.py
+++ b/solution.py
@@ -22,6 +22,10 @@
     return lax.dot_general(left, right, (((1,), (0,)), ((), ())), preferred_element_type=F32)
 
 
+def dot_last(left, right):
+    return lax.dot_general(left, right, (((1,), (1,)), ((), ())), preferred_element_type=F32)
+
+
 def place_outputs(a, b, c, out_a, out_b, out_c):
     out_a[...] = a[...]
     out_b[...] = b[...]
@@ -32,11 +36,11 @@
     n, heads_axis, model_width,
     lens, hid_h, qkg_h, ng_h, freq_h, wqkv_h, ck_h, cv_h, wout_h, wgu_h, wdn_h,
     out, nk, nv,
-    wqkv, ck, cv, wout, wgu, wdn, wout_t, wdn_t, load_sem,
+    wqkv, ck, cv, wout, wgu, wdn, load_sem,
     hid, qkg, ng, freq, small_sem,
     hp, pq, zq, pkv, zkv, rs_send, rs_recv,
     sqs, sqr, sq_send, sq_recv,
-    scores, att, att_send, att_recv,
+    scores, numer, att, att_send, att_recv,
     ar, ar_send, ar_recv,
     pw_src, pw_dst, pw_send, pw_recv,
     hm, gp, gy, gs, gz, gy_send, gy_recv, gz_send, gz_recv,
@@ -140,8 +144,6 @@
     sine = jnp.sin(angles)
     sine = jnp.where(lane < HEAD_DIM // 2, -sine, sine)
 
-    loads[3].wait()
-    wout_t[...] = wout[...].astype(F32).T.astype(BF16)
     small_loads[1].wait()
     query = gathered(pq, zq, zq_copies)
 
@@ -180,22 +182,27 @@
     for h in range(heads):
         inside = (wide_lane >= h * HEAD_DIM) & (wide_lane < (h + 1) * HEAD_DIM)
         q_rows.append(jnp.where(inside, query_rot, 0.0))
-    q_cols = jnp.concatenate(q_rows, axis=0).T.astype(BF16)
+    q_all = jnp.concatenate(q_rows, axis=0).astype(BF16)
     first = jnp.concatenate([starts[:, 0:1]] * heads, axis=0)
     last = jnp.concatenate([ends[:, 0:1]] * heads, axis=0)
     pool = ck.shape[0]
     loads[1].wait()
     q_scale = jnp.concatenate([inverse_root(q_copies, 0) * scale] * heads, axis=0)
-    highest = jnp.full((heads * rows, KEY_BLOCK), -1e30, F32)
     column = lax.broadcasted_iota(jnp.int32, (heads * rows, KEY_BLOCK), 1)
-    for b in range(pool // KEY_BLOCK):
-        span = pl.ds(b * KEY_BLOCK, KEY_BLOCK)
-        s = dot(ck[span, :], q_cols).T * q_scale
-        place = b * KEY_BLOCK + column
+    blocks = pool // KEY_BLOCK
+
+    def score_block(b, highest):
+        start = pl.multiple_of(b * KEY_BLOCK, KEY_BLOCK)
+        span = pl.ds(start, KEY_BLOCK)
+        s = dot_last(q_all, ck[span, :]) * q_scale
+        place = start + column
         s = jnp.where((place >= first) & (place < last), s, -1e30)
-        scores[:, span] = s
-        highest = jnp.maximum(highest, s)
-    highest = jnp.max(highest, axis=1, keepdims=True)
+        scores[b] = s
+        return jnp.maximum(highest, jnp.max(s, axis=1, keepdims=True))
+
+    highest = lax.fori_loop(
+        0, blocks, score_block, jnp.full((heads * rows, 1), -1e30, F32)
+    )
 
     both = gathered(pkv, zkv, zkv_copies)
     key_new = both[:, :width]
@@ -203,15 +210,19 @@
     nv[...] = value_new
     k_copies = share_power(key_new, 1)
 
-    total = jnp.zeros((heads * rows, KEY_BLOCK), F32)
-    numerator = jnp.zeros((heads * rows, width), F32)
     loads[2].wait()
-    for b in range(pool // KEY_BLOCK):
-        span = pl.ds(b * KEY_BLOCK, KEY_BLOCK)
-        w = jnp.exp(scores[:, span] - highest).astype(BF16)
-        total = total + w.astype(F32)
-        numerator = numerator + dot(w, cv[span, :])
-    denominator = jnp.sum(total, axis=1, keepdims=True)
+    numer[...] = jnp.zeros_like(numer)
+
+    def value_block(b, total):
+        span = pl.ds(pl.multiple_of(b * KEY_BLOCK, KEY_BLOCK), KEY_BLOCK)
+        w = jnp.exp(scores[b] - highest).astype(BF16)
+        numer[...] += dot(w, cv[span, :])
+        return total + jnp.sum(w.astype(F32), axis=1, keepdims=True)
+
+    denominator = lax.fori_loop(
+        0, blocks, value_block, jnp.zeros((heads * rows, 1), F32)
+    )
+    numerator = numer[...]
 
     key_rot = rotate(key_new * inverse_root(k_copies, 1) * qkg[1:2, :]).astype(BF16)
     nk[...] = key_rot
@@ -298,7 +309,8 @@
         return jnp.sum(jnp.where(eye, scaled, 0.0), axis=1, keepdims=True)
 
     small_loads[2].wait()
-    attn = sum_heads(dot(att[...].reshape(total_rows, width), wout_t[...]), 0)
+    loads[3].wait()
+    attn = sum_heads(dot_last(att[...].reshape(total_rows, width), wout[...]), 0)
     attn = attn * inverse_rms(attn, 0) * ng[0:1, :]
     hm[...] = (hp[...].astype(F32) + attn).astype(BF16)
 
@@ -314,8 +326,6 @@
             send(gp.at[c, 1 - yi], gy.at[c], gy_send.at[c], gy_recv.at[c], ypart, hi)
         )
     pending += gy_copies
-    loads[5].wait()
-    wdn_t[...] = wdn[...].astype(F32).T.astype(BF16)
     gz_copies = {}
     ay_copies = {}
     az_copies = {}
@@ -361,7 +371,9 @@
             src_ref=other, dst_ref=other, send_sem=ay_send.at[c], recv_sem=ay_recv.at[c],
             device_id=(ypart, hi), device_id_type=MESH,
         ).wait_recv()
-        part = dot(act[c].reshape(total_rows, cu), wdn_t[pl.ds(c * cu, cu), :])
+        if c == 0:
+            loads[5].wait()
+        part = dot_last(act[c].reshape(total_rows, cu), wdn[:, pl.ds(c * cu, cu)])
         state["down"] = part if state["down"] is None else state["down"] + part
 
     stages = (pair_sum, activate, forward, project)
@@ -400,7 +412,7 @@
     scratch = [
         vmem(w_qkv.shape, BF16), vmem(cache_keys.shape, BF16), vmem(cache_values.shape, BF16),
         vmem(w_out.shape, BF16), vmem(w_gate_up.shape, BF16), vmem(w_down.shape, BF16),
-        vmem(w_out.shape[::-1], BF16), vmem(w_down.shape[::-1], BF16), dma((6,)),
+        dma((6,)),
         vmem(hidden_in.shape, BF16), vmem(qk_gain.shape, F32), vmem(norm_gain.shape, F32),
         vmem((8, HEAD_DIM), F32), dma((4,)),
         vmem((total_rows, feat), BF16),
@@ -409,7 +421,8 @@
         dma((2, n - 1)), dma((2, n - 1)),
         vmem((2, rows, HEAD_DIM), F32), vmem((2, heads_axis - 1, rows, HEAD_DIM), F32),
         dma((2, heads_axis - 1)), dma((2, heads_axis - 1)),
-        vmem((heads * rows, cache_keys.shape[0]), F32),
+        vmem((cache_keys.shape[0] // KEY_BLOCK, heads * rows, KEY_BLOCK), F32),
+        vmem((heads * rows, width), F32),
         vmem((n, rows, width), BF16), dma((n - 1,)), dma((n - 1,)),
         vmem((2, heads_axis, total_rows, feat), BF16),
         dma((2, heads_axis - 1)), dma((2, heads_axis - 1)),

time: 76.1 us -> 77.7 us (1.021)
  Pallas kernels: 75.2 us -> 76.9 us
    pallas_call x1, Pallas kernels: 73.7 us -> 75.4 us  [body(): pl.pallas_call(functools.partial(kernel, n, heads_axis, feat * n), out_sh...]
where the time goes in v5:
time: 77.7 us; the launch traced here: 77.5 us
  Pallas kernels  76.9 us (99%)
    pallas_call x1, Pallas kernels, body(): pl.pallas_call(functools.partial(kernel, n, heads_axis, feat * n), out_sh...  75.4 us

profile of v5, /device:TPU:0, one launch (start us, length us, event | category | flops | bytes accessed | tf_op | source)
XLA Modules:
  0.0 77.5 jit_solution(3674960046517914390)
XLA Ops:
  0.6 75.4 %shard_map.130 = (bf16[128,256]{1,0:T(8,128)(2,1)}, bf16[16,512]{1,0:T(8,128)(2,1)}, bf16[16,512]{1,0:T(8,128)(2,1)}) custom-call(s32[16]{0:T(128)} %lens.1, bf16[128,256]{1,0:T(8,128)(2,1)} %hid_h.1, f32[2,512]{1,0:T(2,128)} %qkg_h.1, f32[2,256]{1,0:T(2,128)} %ng_h.1, f32[8,128]{1,0:T(8,128)} %constant.2.clone.freq_h, bf16[3,256,512]{2,1,0:T(8,128)(2,1)} %wqkv_h.1, ...), custom_call_target="tpu_custom_call" | custom-call | tf_op jit(solution)/shard_map/pallas_call | solution.py:440
  76.0 1.5 %shard_map.131 = (bf16[128,256]{1,0:T(8,128)(2,1)}, bf16[16,512]{1,0:T(8,128)(2,1)}, bf16[16,512]{1,0:T(8,128)(2,1)}) custom-call(bf16[128,256]{1,0:T(8,128)(2,1)} %get-tuple-element.6.a, bf16[16,512]{1,0:T(8,128)(2,1)} %get-tuple-element.7.b, bf16[16,512]{1,0:T(8,128)(2,1)} %get-tuple-element.8.c), custom_call_target="tpu_custom_call" | custom-call | tf_op jit(solution)/shard_map/pallas_call | solution.py:457

commit v6 on v3

--- a/solution.py
+++ b/solution.py
@@ -15,6 +15,7 @@
 F32 = jnp.float32
 BF16 = jnp.bfloat16
 CHUNKS = 4
+IN_FLIGHT = 2
 KEY_BLOCK = 512
 
 
@@ -121,7 +122,6 @@
     zq_copies = scatter(pq, zq, 0)
     pkv[:, :, :width] = dot(x, wqkv[1]).astype(BF16).reshape(n, rows, width)
     pkv[:, :, width:] = dot(x, wqkv[2]).astype(BF16).reshape(n, rows, width)
-    zkv_copies = scatter(pkv, zkv, 1)
 
     row_id = lax.broadcasted_iota(jnp.int32, (rows, HEAD_DIM), 0)
     lane = lax.broadcasted_iota(jnp.int32, (rows, HEAD_DIM), 1)
@@ -172,6 +172,7 @@
         return jnp.concatenate(parts, axis=1)
 
     q_copies = share_power(query, 0)
+    zkv_copies = scatter(pkv, zkv, 1)
     query_rot = rotate(query * qkg[0:1, :]).astype(BF16).astype(F32)
 
     scale = HEAD_DIM ** (-0.5)
@@ -246,6 +247,8 @@
             send(att.at[slot], att.at[slot], att_send.at[d - 1], att_recv.at[d - 1], t, hi)
         )
     pending += att_copies
+    loads[5].wait()
+    wdn_t[...] = wdn[...].astype(F32).T.astype(BF16)
     for d in range(1, n):
         s = lax.rem(me - d + n, n)
         there = att.at[lax.rem(s, 2) * m + lax.div(s, 2)]
@@ -305,17 +308,17 @@
     units = wgu.shape[2]
     cu = units // CHUNKS
     loads[4].wait()
-    gy_copies = []
-    for c in range(CHUNKS):
+    gy_copies = {}
+
+    def launch(c):
         cols = pl.ds(c * cu, cu)
         gp[c, :, :, :, :cu] = dot(hm[...], wgu[0, :, cols]).astype(BF16).reshape(2, m, rows, cu)
         gp[c, :, :, :, cu:] = dot(hm[...], wgu[1, :, cols]).astype(BF16).reshape(2, m, rows, cu)
-        gy_copies.append(
-            send(gp.at[c, 1 - yi], gy.at[c], gy_send.at[c], gy_recv.at[c], ypart, hi)
-        )
-    pending += gy_copies
-    loads[5].wait()
-    wdn_t[...] = wdn[...].astype(F32).T.astype(BF16)
+        gy_copies[c] = send(gp.at[c, 1 - yi], gy.at[c], gy_send.at[c], gy_recv.at[c], ypart, hi)
+        pending.append(gy_copies[c])
+
+    for c in range(IN_FLIGHT):
+        launch(c)
     gz_copies = {}
     ay_copies = {}
     az_copies = {}
@@ -329,6 +332,8 @@
             gz_copies[c, d] = send(gs.at[c, t], gz.at[c, d - 1], gz_send.at[c, d - 1],
                                    gz_recv.at[c, d - 1], t * 2 + yi, hi)
             pending.append(gz_copies[c, d])
+        if c + IN_FLIGHT < CHUNKS:
+            launch(c + IN_FLIGHT)
 
     def activate(c):
         full = gs[c, zi].astype(F32)

time: 76.1 us -> 75 us (0.986)
  Pallas kernels: 75.2 us -> 74.1 us
    pallas_call x1, Pallas kernels: 73.7 us -> 72.6 us  [body(): pl.pallas_call(functools.partial(kernel, n, heads_axis, feat * n), out_sh...]
where the time goes in v6:
time: 75 us; the launch traced here: 74.8 us
  Pallas kernels  74.1 us (99%)
    pallas_call x1, Pallas kernels, body(): pl.pallas_call(functools.partial(kernel, n, heads_axis, feat * n), out_sh...  72.6 us

profile of v6, /device:TPU:0, one launch (start us, length us, event | category | flops | bytes accessed | tf_op | source)
XLA Modules:
  0.0 74.8 jit_solution(13486370877313516093)
XLA Ops:
  0.6 72.6 %shard_map.130 = (bf16[128,256]{1,0:T(8,128)(2,1)}, bf16[16,512]{1,0:T(8,128)(2,1)}, bf16[16,512]{1,0:T(8,128)(2,1)}) custom-call(s32[16]{0:T(128)} %lens.1, bf16[128,256]{1,0:T(8,128)(2,1)} %hid_h.1, f32[2,512]{1,0:T(2,128)} %qkg_h.1, f32[2,256]{1,0:T(2,128)} %ng_h.1, f32[8,128]{1,0:T(8,128)} %constant.2.clone.freq_h, bf16[3,256,512]{2,1,0:T(8,128)(2,1)} %wqkv_h.1, ...), custom_call_target="tpu_custom_call" | custom-call | tf_op jit(solution)/shard_map/pallas_call | solution.py:432
  73.3 1.5 %shard_map.131 = (bf16[128,256]{1,0:T(8,128)(2,1)}, bf16[16,512]{1,0:T(8,128)(2,1)}, bf16[16,512]{1,0:T(8,128)(2,1)}) custom-call(bf16[128,256]{1,0:T(8,128)(2,1)} %get-tuple-element.6.a, bf16[16,512]{1,0:T(8,128)(2,1)} %get-tuple-element.7.b, bf16[16,512]{1,0:T(8,128)(2,1)} %get-tuple-element.8.c), custom_call_target="tpu_custom_call" | custom-call | tf_op jit(solution)/shard_map/pallas_call | solution.py:449

commit v7 on v6

--- a/solution.py
+++ b/solution.py
@@ -14,8 +14,8 @@
 MESH = pl.DeviceIdType.MESH
 F32 = jnp.float32
 BF16 = jnp.bfloat16
-CHUNKS = 4
-IN_FLIGHT = 2
+CHUNKS = 2
+IN_FLIGHT = 1
 KEY_BLOCK = 512
 
 

time: 75 us -> 78 us (1.040)
  Pallas kernels: 74.1 us -> 77.2 us
    pallas_call x1, Pallas kernels: 72.6 us -> 75.7 us  [body(): pl.pallas_call(functools.partial(kernel, n, heads_axis, feat * n), out_sh...]
where the time goes in v7:
time: 78 us; the launch traced here: 77.8 us
  Pallas kernels  77.2 us (99%)
    pallas_call x1, Pallas kernels, body(): pl.pallas_call(functools.partial(kernel, n, heads_axis, feat * n), out_sh...  75.7 us

profile of v7, /device:TPU:0, one launch (start us, length us, event | category | flops | bytes accessed | tf_op | source)
XLA Modules:
  0.0 77.8 jit_solution(14442190835836921493)
XLA Ops:
  0.6 75.7 %shard_map.130 = (bf16[128,256]{1,0:T(8,128)(2,1)}, bf16[16,512]{1,0:T(8,128)(2,1)}, bf16[16,512]{1,0:T(8,128)(2,1)}) custom-call(s32[16]{0:T(128)} %lens.1, bf16[128,256]{1,0:T(8,128)(2,1)} %hid_h.1, f32[2,512]{1,0:T(2,128)} %qkg_h.1, f32[2,256]{1,0:T(2,128)} %ng_h.1, f32[8,128]{1,0:T(8,128)} %constant.2.clone.freq_h, bf16[3,256,512]{2,1,0:T(8,128)(2,1)} %wqkv_h.1, ...), custom_call_target="tpu_custom_call" | custom-call | tf_op jit(solution)/shard_map/pallas_call | solution.py:432
  76.3 1.5 %shard_map.131 = (bf16[128,256]{1,0:T(8,128)(2,1)}, bf16[16,512]{1,0:T(8,128)(2,1)}, bf16[16,512]{1,0:T(8,128)(2,1)}) custom-call(bf16[128,256]{1,0:T(8,128)(2,1)} %get-tuple-element.6.a, bf16[16,512]{1,0:T(8,128)(2,1)} %get-tuple-element.7.b, bf16[16,512]{1,0:T(8,128)(2,1)} %get-tuple-element.8.c), custom_call_target="tpu_custom_call" | custom-call | tf_op jit(solution)/shard_map/pallas_call | solution.py:449
